TPU v7x, 512 devices: a whole 4x4x16 slice. The times are simulated.
512 devices in a mesh: row: 32 (over z_lo, x), col: 16 (over y, z_hi, core).
Axes of the slice: x: 4, y: 4, z: 16 (z_hi: 2, z_lo: 8; z = z_hi * 8 + z_lo), core: 2. Of those that a mesh axis runs over, the one named last changes fastest.
Arguments:
- queries: bfloat16 [49152, 128], P(('row', 'col')), may hold values from -6 to 6
- key_vectors: bfloat16 [49152, 128], P(('col', 'row')), may hold values from -6 to 6
- value_vectors: bfloat16 [49152, 128], P(('col', 'row')), may hold values from -6 to 6
- outputs: bfloat16 [49152, 128], P(('row', 'col')), may hold values from -3 to 3
- out_grad: bfloat16 [49152, 128], P(('row', 'col')), may hold values from -1.796875 to 1.796875
- logsumexp: float32 [49152], P(('row', 'col')), may hold values from -0.5 to 13
- positions: int32 [49152], P(('row', 'col')), may hold values from 0 to 49151, as said below
Outputs:
- query_grad: bfloat16 [49152, 128], P(('row', 'col'))
- key_grad: bfloat16 [49152, 128], P(('col', 'row'))
- value_grad: bfloat16 [49152, 128], P(('col', 'row'))
Inputs may be any that keep to these rules, and one draw needn't show every extreme that they name: positions is a permutation of the token positions; the slots of one device hold position block m and then block 1023 - m, each of 48 consecutive positions in increasing order, for a block number m that differs from device to device.
All inputs are finite; a program needn't handle non-finite values.
Results may differ from a plain program's by a relative error of at most 0.007.
Values may be sent and summed in bfloat16 or wider, within the bound.
A program may use at most 64 MiB of HBM per device.

v0:
```python
import math

import jax
import jax.numpy as jnp
from jax import lax
from jax.sharding import PartitionSpec as P


def block_grads_keyed(
    query_block, dout_block, saved_lse, row_delta, query_pos, key_block, value_block, key_pos
):
    scaling = query_block.shape[1] ** (-0.5)
    scores_keyed = jnp.dot(key_block, query_block.T, preferred_element_type=jnp.float32) * scaling
    allowed = key_pos[:, None] <= query_pos[None, :]
    probs_full = jnp.where(allowed, jnp.exp(scores_keyed - saved_lse[None, :]), jnp.float32(0.0))
    probs_half = probs_full.astype(jnp.bfloat16)
    dprobs = jnp.dot(value_block, dout_block.T, preferred_element_type=jnp.float32)
    dscores = (scaling * probs_full * (dprobs - row_delta[None, :])).astype(jnp.bfloat16)
    grad_query = jnp.dot(dscores.T, key_block, preferred_element_type=jnp.float32)
    grad_key = jnp.dot(dscores, query_block, preferred_element_type=jnp.float32)
    grad_value = jnp.dot(probs_half, dout_block, preferred_element_type=jnp.float32)
    return (grad_query, grad_key, grad_value)


def make_folder(query_block, dout_block, saved_lse, row_delta, query_pos, key_pos):
    width = query_block.shape[1]

    def fold_keys(carry, pieces, start):
        query_total, key_total, value_total = carry
        key_piece, value_piece = pieces
        piece_rows = key_piece.shape[0]
        sub_rows = math.gcd(piece_rows, 384)
        sub_count = piece_rows // sub_rows

        def advance(running, inputs_block):
            key_sub, value_sub, pos_sub = inputs_block
            grad_query, grad_key, grad_value = block_grads_keyed(
                query_block,
                dout_block,
                saved_lse,
                row_delta,
                query_pos,
                key_sub,
                value_sub,
                pos_sub,
            )
            return (running + grad_query, (grad_key, grad_value))

        stacked = (
            key_piece.reshape(sub_count, sub_rows, width),
            value_piece.reshape(sub_count, sub_rows, width),
            key_pos.reshape(sub_count, sub_rows),
        )
        query_total, (key_parts, value_parts) = lax.scan(advance, query_total, stacked)
        key_total = key_parts.reshape(piece_rows, width)
        value_total = value_parts.reshape(piece_rows, width)
        return (query_total, key_total, value_total)

    return fold_keys


def shards(queries, key_vectors, value_vectors, outputs, out_grad, logsumexp, positions):
    shard_rows = queries.shape[0]
    width = queries.shape[1]
    row_delta = jnp.sum(out_grad.astype(jnp.float32) * outputs.astype(jnp.float32), axis=1)
    all_slots = lax.all_gather(positions, ("row", "col"), axis=0, tiled=True)
    n_row = lax.axis_size("row")
    n_col = lax.axis_size("col")
    row_id = lax.axis_index("row")
    col_id = lax.axis_index("col")
    query_grid = all_slots.reshape(n_row, n_col, shard_rows)
    key_grid = all_slots.reshape(n_col, n_row, shard_rows)
    query_block, dout_block = (
        lax.all_gather(queries, "col", axis=0, tiled=True),
        lax.all_gather(out_grad, "col", axis=0, tiled=True),
    )
    saved_lse, delta_block = (
        lax.all_gather(logsumexp, "col", axis=0, tiled=True),
        lax.all_gather(row_delta, "col", axis=0, tiled=True),
    )
    query_pos = lax.dynamic_index_in_dim(query_grid, row_id, 0, keepdims=False).reshape(-1)
    key_pos = lax.dynamic_index_in_dim(key_grid, col_id, 0, keepdims=False).reshape(-1)
    key_total_rows = shard_rows * n_row
    folder = make_folder(query_block, dout_block, saved_lse, delta_block, query_pos, key_pos)
    initial = (
        jnp.zeros((query_block.shape[0], width), jnp.float32),
        jnp.zeros((key_total_rows, width), jnp.float32),
        jnp.zeros((key_total_rows, width), jnp.float32),
    )
    query_part, key_part, value_part = folder(
        initial,
        (
            lax.all_gather(key_vectors, "row", axis=0, tiled=True),
            lax.all_gather(value_vectors, "row", axis=0, tiled=True),
        ),
        jnp.int32(0),
    )
    query_sum = lax.psum_scatter(query_part, "col", scatter_dimension=0, tiled=True)
    key_sum, value_sum = (
        lax.psum_scatter(key_part, "row", scatter_dimension=0, tiled=True),
        lax.psum_scatter(value_part, "row", scatter_dimension=0, tiled=True),
    )
    return (
        query_sum.astype(jnp.bfloat16),
        key_sum.astype(jnp.bfloat16),
        value_sum.astype(jnp.bfloat16),
    )


def solution(mesh):
    in_specs = (
        P(("row", "col"), None),
        P(("col", "row"), None),
        P(("col", "row"), None),
        P(("row", "col"), None),
        P(("row", "col"), None),
        P(("row", "col")),
        P(("row", "col")),
    )
    out_specs = (P(("row", "col"), None), P(("col", "row"), None), P(("col", "row"), None))
    return jax.shard_map(shards, mesh=mesh, in_specs=in_specs, out_specs=out_specs, check_vma=False)
```

profile of v0, /device:TPU:16, one launch (start us, length us, event | category | flops | bytes accessed | tf_op | source)
XLA Modules:
  0.0 1132.9 jit_solution(3750423538623608744)
XLA Ops:
  10.2 53.8 %all_gather.26 = bf16[1536,128]{1,0:T(8,128)(2,1)} all-gather(bf16[96,128]{1,0:T(8,128)(2,1)} %param.13), channel_id=1, replica_groups=mesh['row'=32,'col'=16] {'col'}, dimensions={0}, use_global_device_ids=true | all-gather | bytes 417792 | tf_op jit(solution)/shard_map/all_gather | solution.py:75
  64.8 119.8 %all_gather.22 = bf16[3072,128]{1,0:T(8,128)(2,1)S(1)} all-gather(bf16[96,128]{1,0:T(8,128)(2,1)} %param.10), channel_id=1, replica_groups=mesh['row'=32,'col'=16] {'row'}, dimensions={0}, use_global_device_ids=true | all-gather | bytes 811008 | tf_op jit(solution)/shard_map/all_gather | solution.py:93
  184.6 120.5 %all_gather.25 = bf16[3072,128]{1,0:T(8,128)(2,1)} all-gather(bf16[96,128]{1,0:T(8,128)(2,1)S(1)} %copy-done.8), channel_id=1, replica_groups=mesh['row'=32,'col'=16] {'row'}, dimensions={0}, use_global_device_ids=true | all-gather | bytes 811008 | tf_op jit(solution)/shard_map/all_gather | solution.py:94
  306.3 114.1 %all-reduce.3 = (f32[1536]{0:T(1024)}, f32[1536]{0:T(1024)S(1)}) all-reduce(f32[1536]{0:T(1024)S(1)} %dynamic-update-slice.1, f32[1536]{0:T(1024)S(1)} %dynamic-update-slice.2), channel_id=1, replica_groups=mesh['row'=32,'col'=16] {'col'}, use_global_device_ids=true, to_apply=%add.1 | all-reduce | flops 3072 | bytes 24576
  420.5 42.1 %all_gather.23 = bf16[1536,128]{1,0:T(8,128)(2,1)S(1)} all-gather(bf16[96,128]{1,0:T(8,128)(2,1)S(1)} %copy-done.9), channel_id=1, replica_groups=mesh['row'=32,'col'=16] {'col'}, dimensions={0}, use_global_device_ids=true | all-gather | bytes 417792 | tf_op jit(solution)/shard_map/all_gather | solution.py:74
  462.6 11.5 %all-reduce.6.cloned.1.call-done = s32[49152]{0:T(1024)} async-done(((s32[49152]{0:T(1024)}), s32[49152]{0:T(1024)}) %all-reduce.6.cloned.1.call-update) | async-done | bytes 196624
  477.6 76.6 %while.16 = (s32[]{:T(128)}, f32[1536,128]{1,0:T(8,128)}, f32[8,384,128]{2,1,0:T(8,128)}, f32[8,384,128]{2,1,0:T(8,128)}, s32[8,384]{1,0:T(8,128)}, /*index=5*/s...) while((s32[]{:T(128)}, f32[1536,128]{1,0:T(8,128)}, ...), condition=%wide.wide.region_2.3_spmd.clone, body=%wide.wide.region_1.2_spmd.clone.sunk | while | flops 760676352 | bytes 27059528 | solution.py:54
  481.1 2.1 fusion.69
  483.3 2.4 convolution_add_fusion.3
  487.6 1.4 fusion.67
  490.4 2.1 fusion.69
  492.6 2.6 convolution_add_fusion.3
  497.2 1.4 fusion.67
  500.0 2.2 fusion.69
  502.2 2.6 convolution_add_fusion.3
  509.6 2.1 fusion.69
  511.8 2.6 convolution_add_fusion.3
  516.4 1.4 fusion.67
  519.2 2.1 fusion.69
  521.4 2.6 convolution_add_fusion.3
  528.8 2.2 fusion.69
  531.0 2.6 convolution_add_fusion.3
  538.5 2.2 fusion.69
  540.6 2.6 convolution_add_fusion.3
  548.1 2.2 fusion.69
  550.2 2.6 convolution_add_fusion.3
  555.5 95.7 %reduce-scatter.4.cloned.1.call-done = f32[96,128]{1,0:T(8,128)} async-done(((f32[1536,128]{1,0:T(8,128)}), f32[96,128]{1,0:T(8,128)}) %reduce-scatter.4.cloned.1.call-update) | async-done | bytes 49168 | tf_op jit(solution)/shard_map/reduce_scatter | solution.py:98
  651.1 1.4 convert_element_type.23
  652.5 236.2 %reduce-scatter.6.cloned.1.call-done = f32[96,128]{1,0:T(8,128)} async-done(((f32[3072,128]{1,0:T(8,128)}), f32[96,128]{1,0:T(8,128)}) %reduce-scatter.6.cloned.1.call-update) | async-done | bytes 49168 | tf_op jit(solution)/shard_map/reduce_scatter | solution.py:100
  888.7 1.4 convert_element_type.24
  890.1 234.8 %reduce-scatter.8.cloned.1.call-done = f32[96,128]{1,0:T(8,128)} async-done(((f32[3072,128]{1,0:T(8,128)}), f32[96,128]{1,0:T(8,128)}) %reduce-scatter.8.cloned.1.call-update) | async-done | bytes 49168 | tf_op jit(solution)/shard_map/reduce_scatter | solution.py:101
  1124.9 1.4 convert_element_type.25
  (160 shorter events, 43.0 us)
Async XLA Ops:
  7.2 177.5 %copy-start.8 = (bf16[96,128]{1,0:T(8,128)(2,1)S(1)}, bf16[96,128]{1,0:T(8,128)(2,1)}, u32[]{:S(2)}) copy-start(bf16[96,128]{1,0:T(8,128)(2,1)} %param.11) | copy-start | bytes 73732
  7.2 298.9 %copy-start.10 = (f32[96]{0:T(128)S(1)}, f32[96]{0:T(128)}, u32[]{:S(2)}) copy-start(f32[96]{0:T(128)} %param.14) | copy-start | bytes 1156
  7.2 413.3 %copy-start.9 = (bf16[96,128]{1,0:T(8,128)(2,1)S(1)}, bf16[96,128]{1,0:T(8,128)(2,1)}, u32[]{:S(2)}) copy-start(bf16[96,128]{1,0:T(8,128)(2,1)} %param.9) | copy-start | bytes 73732
  7.2 466.9 %all-reduce.6.cloned.1.call-start = ((), (), s32[]{:S(2)}) async-start(), calls=%async_computation.6 | async-start | bytes 393216
  8.9 642.3 %reduce-scatter.4.cloned.1.call-start = ((), (), s32[]{:S(2)}) async-start(), calls=%async_computation.3 | async-start | bytes 835584 | tf_op jit(solution)/shard_map/reduce_scatter | solution.py:98
  475.1 2.4 copy-start.7
  477.6 2.1 copy-start.2
  477.6 2.2 copy-start.4
  483.3 2.4 copy-start.1
  486.9 2.2 copy-start.2
  486.9 2.2 copy-start.4
  492.6 2.6 copy-start.1
  496.5 2.2 copy-start.2
  496.5 2.2 copy-start.4
  502.2 2.6 copy-start.1
  506.1 2.1 copy-start.2
  506.1 2.2 copy-start.4
  511.8 2.6 copy-start.1
  515.7 2.2 copy-start.2
  515.7 2.2 copy-start.4
  521.4 2.6 copy-start.1
  525.3 2.2 copy-start.2
  525.3 2.2 copy-start.4
  531.0 2.6 copy-start.1
  534.9 2.2 copy-start.2
  534.9 2.2 copy-start.4
  540.6 2.6 copy-start.1
  544.5 2.2 copy-start.2
  544.5 2.2 copy-start.4
  550.2 2.6 copy-start.1
  554.1 334.6 %reduce-scatter.6.cloned.1.call-start = ((), (), s32[]{:S(2)}) async-start(), calls=%async_computation.4 | async-start | bytes 1622016 | tf_op jit(solution)/shard_map/reduce_scatter | solution.py:100
  554.9 570.1 %reduce-scatter.8.cloned.1.call-start = ((), (), s32[]{:S(2)}) async-start(), calls=%async_computation.5 | async-start | bytes 1622016 | tf_op jit(solution)/shard_map/reduce_scatter | solution.py:101
  (25 other events, 31.6 us)
Sparse Core Ops, SparseCore 0:
  13.5 460.5 all-reduce.5
  554.3 96.8 reduce-scatter.3
  654.1 234.4 reduce-scatter.5
  891.3 233.5 reduce-scatter.7
where the time goes:
time: 1140 us; the launch traced here: 1130 us
  waiting for transfers between devices  579 us (51%)
  blocking collectives  450 us (39%)
  matrix products  69.5 us (6%)
  between operations  14.5 us (1%)
  local copies, waits for them, and re-layouts  13.5 us (1%)
    reduce_scatter x1, waiting for transfers between devices, shards(): lax.psum_scatter(key_part, 'row', scatter_dimension=0, tiled=True)  236 us
    reduce_scatter x1, waiting for transfers between devices, shards(): lax.psum_scatter(value_part, 'row', scatter_dimension=0, tiled=True)  235 us
    all_gather x1, blocking collectives, shards(): lax.all_gather(value_vectors, 'row', axis=0, tiled=True)  121 us
    all_gather x1, blocking collectives, shards(): lax.all_gather(key_vectors, 'row', axis=0, tiled=True)  120 us
    unnamed x1, blocking collectives  114 us
    reduce_scatter x1, waiting for transfers between devices, shards(): lax.psum_scatter(query_part, 'col', scatter_dimension=0, tiled=True)  95.7 us
    all_gather x1, blocking collectives, shards(): lax.all_gather(out_grad, 'col', axis=0, tiled=True)  53.8 us
    all_gather x1, blocking collectives, shards(): lax.all_gather(queries, 'col', axis=0, tiled=True)  42.1 us
  transfers between devices with their start and end apart: 4, of which 4 were waited for; matrix products, arithmetic and copies ran while one was open for 0% of the time, Pallas kernels for 0%

commit v1 on v0

v1 whole, which is shorter than its diff:
```python
import functools

import jax
import jax.numpy as jnp
from jax import lax
from jax.experimental import pallas as pl
from jax.experimental.pallas import tpu as pltpu
from jax.sharding import PartitionSpec as P

MESH = pl.DeviceIdType.MESH
F32 = jnp.float32
BF16 = jnp.bfloat16
NT = (((1,), (1,)), ((), ()))
NN = (((1,), (0,)), ((), ()))
TN = (((0,), (0,)), ((), ()))
LOG2E = 1.4426950408889634

ROUNDS = ((0, -1, 1, 2), (-2, 3, -3, 4), (-4, 5, -5, 6), (-6, 7, -7, 8))
ROUND_OF = {o: r for r, offs in enumerate(ROUNDS) for o in offs}
PLANE = [(a, b) for a in range(4) for b in range(4) if (a, b) != (0, 0)]


def dot(a, b, dims):
    return lax.dot_general(a, b, dims, preferred_element_type=F32)


def device(x, y, z, core):
    return (lax.rem(z, 8) * 4 + x, (y * 2 + z // 8) * 2 + core)


def kernel(
    half, q_ref, k_ref, v_ref, o_ref, do_ref, lse_ref, pos_ref,
    gq_ref, gk_ref, gv_ref,
    qbuf, kbuf, rowbuf, mrow, mbuf, pk, rows, dq, dk, dv,
    sib_out, sib_in, dq_out, dq_in, kv_out, kv_in,
    send_sem, q_recv, qs_recv, k_recv, m_recv, mb_recv, sib_recv, dq_recv, kv_recv,
):
    width = q_ref.shape[1]
    shard = 2 * half
    scale = width ** -0.5
    row, col = lax.axis_index("row"), lax.axis_index("col")
    z_lo, x = row // 4, lax.rem(row, 4)
    core, z_hi, y = lax.rem(col, 2), lax.rem(col // 2, 2), col // 4
    z = z_hi * 8 + z_lo
    other = 1 - core

    def at_z(o):
        return device(x, y, lax.rem(z + o + 16, 16), core)

    def at_plane(a, b):
        return device(lax.rem(x + a, 4), lax.rem(y + b, 4), z, core)

    sibling = device(x, y, z, other)

    to_z = lax.rem(z, 2) * 8 + lax.rem(x, 2) * 4 + y
    to_core = x // 2
    to_self = jnp.logical_and(to_z == z, to_core == core)
    my_mslot = (z_hi * 2 + core) * 4 + z_lo // 2
    collects = jnp.logical_and(x == core * 2 + z_lo // 4, y == lax.rem(z_lo, 4))

    def holder(slot):
        xo, yo = slot // 4, slot % 4
        hz, hc = (xo // 2) * 8 + 2 * yo + z_hi, xo % 2
        return hz, hc, jnp.logical_and(hz == z, hc == core)

    barrier = pltpu.get_barrier_semaphore()
    for o in range(1, 16):
        pl.semaphore_signal(barrier, inc=1, device_id=at_z(o), device_id_type=MESH)
    for a, b in PLANE:
        pl.semaphore_signal(barrier, inc=1, device_id=at_plane(a, b), device_id_type=MESH)
    pl.semaphore_signal(barrier, inc=1, device_id=sibling, device_id_type=MESH)
    for slot in range(16):
        hz, hc, mine = holder(slot)

        @pl.when(jnp.logical_and(collects, jnp.logical_not(mine)))
        def _():
            pl.semaphore_signal(
                barrier, inc=1, device_id=device(x, y, hz, hc), device_id_type=MESH
            )

    sends = []

    def send(src, dst, recv_sem, target):
        cp = pltpu.make_async_remote_copy(
            src_ref=src, dst_ref=dst, send_sem=send_sem.at[len(sends)], recv_sem=recv_sem,
            device_id=target, device_id_type=MESH,
        )
        sends.append(cp)
        cp.start()

    def arrived(dst, recv_sem):
        pltpu.make_async_remote_copy(
            src_ref=dst, dst_ref=dst, send_sem=send_sem.at[0], recv_sem=recv_sem,
            device_id=sibling, device_id_type=MESH,
        ).wait_recv()

    my_qslot = lax.rem(z, 4) * 2 + core
    my_kslot = x * 4 + y
    qbuf[0, my_qslot, 0:shard] = q_ref[...]
    qbuf[0, my_qslot, shard:2 * shard] = do_ref[...]
    kbuf[my_kslot, 0:shard] = k_ref[...]
    kbuf[my_kslot, shard:2 * shard] = v_ref[...]
    prod = do_ref[...].astype(F32) * o_ref[...].astype(F32)
    rowbuf[...] = jnp.zeros_like(rowbuf)
    rowbuf[0:1, 0:shard] = lse_ref[...] * LOG2E
    rowbuf[1:2, 0:shard] = jnp.sum(prod.T, axis=0, keepdims=True)
    base = jnp.broadcast_to(pos_ref[0:1, 0:1].astype(F32), (1, 128))
    mrow[...] = base
    shift = lax.rem(my_qslot * half, 128)
    early = pltpu.roll(rowbuf[...], shift, 1)
    late = pltpu.roll(rowbuf[...], lax.rem(shift + 128 - half, 128), 1)
    sub = lax.broadcasted_iota(jnp.int32, (8, 128), 0)
    full = jnp.where(
        sub < 2, early,
        jnp.where(sub < 4, pltpu.roll(late, 2, 0), jnp.where(sub == 4, jnp.broadcast_to(base, (8, 128)), 0.0)),
    )
    hi = full.astype(BF16).astype(F32)
    mid = (full - hi).astype(BF16).astype(F32)
    low = full - hi - mid
    parts = jnp.concatenate([hi, mid, low, jnp.zeros_like(hi)], axis=0)
    qbuf[0, my_qslot, 2 * shard:2 * shard + 32] = parts.astype(BF16)

    pl.semaphore_wait(barrier, 31 + jnp.where(to_self, 0, 1))

    def qslot(o):
        return lax.rem(z + o + 16, 4) * 2 + core

    def sslot(o):
        return lax.rem(z + o + 16, 4) * 2 + other

    def relay(o):
        src = qbuf.at[ROUND_OF[o], qslot(o)]
        for sign in ((1, -1) if o == 0 else ((1,) if o < 0 else (-1,))):
            for d in (2, 1):
                there = o - sign * d
                if there in ROUND_OF and abs(there) <= 8:
                    send(src, qbuf.at[ROUND_OF[there], qslot(o)], q_recv.at[there + 7], at_z(sign * d))

    def to_sibling(o):
        ref = qbuf.at[ROUND_OF[o], qslot(o)]
        send(ref, ref, qs_recv.at[o + 7], sibling)

    def take(o):
        arrived(qbuf.at[ROUND_OF[o], qslot(o)], q_recv.at[o + 7])

    relay(0)
    to_sibling(0)
    for i, (a, b) in enumerate(PLANE):
        ref = kbuf.at[my_kslot]
        send(ref, ref, k_recv.at[i], at_plane(a, b))

    m_copy = pltpu.make_async_remote_copy(
        src_ref=mrow, dst_ref=mbuf.at[my_mslot], send_sem=send_sem.at[send_sem.shape[0] - 1],
        recv_sem=m_recv.at[my_mslot], device_id=device(x, y, to_z, to_core), device_id_type=MESH,
    )

    @pl.when(jnp.logical_not(to_self))
    def _():
        m_copy.start()

    @pl.when(to_self)
    def _():
        mbuf[my_mslot] = mrow[...]

    lane = lax.broadcasted_iota(jnp.int32, (8, 128), 1)

    def unpack(r):
        tiles = []
        pieces = []
        for s in range(8):
            raw = qbuf[r, s, 2 * shard:2 * shard + 32].astype(F32)
            pieces.append(raw[0:8] + raw[8:16] + raw[16:24])
        for j in range(8 * half // 128):
            first, last = 128 * j // half, (128 * j + 127) // half
            tile = pieces[last]
            for s in range(last - 1, first - 1, -1):
                tile = jnp.where(lane < (s + 1) * half - 128 * j, pieces[s], tile)
            tiles.append(tile)
        rows[r] = jnp.concatenate(tiles, axis=1)

    nq = 8 * half
    nk = 8 * half
    lanes = lax.broadcasted_iota(jnp.int32, (1, nq), 1).astype(F32)
    offs = lanes - half * jnp.floor((lanes + 0.5) * (1.0 / half))
    top = 1023.0 * half

    def block(r, kh, qh, kb, masked, first_q, first_k):
        k = kbuf[8 * kb:8 * kb + 8, kh * half:(kh + 1) * half].reshape(nk, width)
        v = kbuf[8 * kb:8 * kb + 8, shard + kh * half:shard + (kh + 1) * half].reshape(nk, width)
        q = qbuf[r, :, qh * half:(qh + 1) * half].reshape(nq, width)
        do = qbuf[r, :, shard + qh * half:shard + (qh + 1) * half].reshape(nq, width)
        lse = rows[r, 2 * qh:2 * qh + 1]
        delta = rows[r, 2 * qh + 1:2 * qh + 2]
        s = dot(k, q, NT)
        dp = dot(v, do, NT)
        p = jnp.exp2(s * (scale * LOG2E) - lse)
        if masked:
            start = rows[r, 4:5]
            pq = (start if qh == 0 else top - start) + offs
            pkk = jnp.concatenate([pk[kh, nk * kb:nk * (kb + 1)]] * (nq // 128), axis=1)
            p = jnp.where(pkk <= pq, p, 0.0)
        ds = (p * (dp - delta)).astype(BF16)
        ph = p.astype(BF16)
        gv, gk, gq = dot(ph, do, NN), dot(ds, q, NN), dot(ds, k, TN)
        span = slice(nk * kb, nk * (kb + 1))
        if first_k:
            dv[kh, span] = gv
            dk[kh, span] = gk
        else:
            dv[kh, span] += gv
            dk[kh, span] += gk
        gq = gq.reshape(8, half, width)
        if first_q:
            dq[r, qh] = gq
        else:
            dq[r, qh] += gq

    def late_early(r, first):
        for kb in range(2):
            block(r, 0, 1, kb, False, kb == 0, first)

    def diagonal(r, first):
        for kb in range(2):
            block(r, 0, 0, kb, True, kb == 0, False)
        for kb in range(2):
            block(r, 1, 1, kb, True, False, first)

    def ready(r):
        for o in ROUNDS[r]:
            arrived(qbuf.at[r, sslot(o)], qs_recv.at[o + 7])
        unpack(r)

    def stage(k):
        for o in (-2 * k, 2 * k):
            if o in ROUND_OF:
                take(o)
                if k < 4:
                    relay(o)
                to_sibling(o)
        for o in (-2 * k + 1, 2 * k - 1):
            take(o)
            to_sibling(o)

    stage(1)
    ready(0)
    for i, (a, b) in enumerate(PLANE):
        arrived(kbuf.at[lax.rem(x - a + 4, 4) * 4 + lax.rem(y - b + 4, 4)], k_recv.at[i])
    late_early(0, True)
    stage(2)

    for slot in range(16):
        hz, hc, mine = holder(slot)

        @pl.when(jnp.logical_and(collects, jnp.logical_not(mine)))
        def _():
            arrived(mbuf.at[slot], m_recv.at[slot])

    mb_copies = [
        pltpu.make_async_remote_copy(
            src_ref=mbuf, dst_ref=mbuf, send_sem=send_sem.at[send_sem.shape[0] - 2 - i],
            recv_sem=mb_recv.at[0], device_id=at_plane(a, b), device_id_type=MESH,
        )
        for i, (a, b) in enumerate(PLANE)
    ]

    @pl.when(collects)
    def _():
        for cp in mb_copies:
            cp.start()

    ready(1)
    late_early(1, False)
    stage(3)
    ready(2)
    late_early(2, False)
    stage(4)
    ready(3)
    late_early(3, False)

    @pl.when(jnp.logical_not(collects))
    def _():
        arrived(mbuf, mb_recv.at[0])

    sub48 = lax.broadcasted_iota(jnp.int32, (half, 128), 0).astype(F32)
    for slot in range(16):
        start = jnp.broadcast_to(mbuf[slot], (half, 128))
        pk[0, slot * half:(slot + 1) * half] = start + sub48
        pk[1, slot * half:(slot + 1) * half] = top - start + sub48

    def share(r):
        for i, o in enumerate(ROUNDS[r]):
            sib_out[r, i, 0:half] = dq[r, 0, sslot(o)].astype(BF16)
            sib_out[r, i, half:shard] = dq[r, 1, sslot(o)].astype(BF16)
        send(sib_out.at[r], sib_in.at[r], sib_recv.at[r], sibling)

    def home(r):
        arrived(sib_in.at[r], sib_recv.at[r])
        for i, o in enumerate(ROUNDS[r]):
            for h in range(2):
                span = slice(h * half, (h + 1) * half)
                total = dq[r, h, qslot(o)] + sib_in[r, i, span].astype(F32)
                if o == 0:
                    dq[r, h, qslot(o)] = total
                else:
                    dq_out[r, i, span] = total.astype(BF16)
            if o != 0:
                send(dq_out.at[r, i], dq_in.at[o + 7], dq_recv.at[o + 7], at_z(o))

    diagonal(3, True)
    share(3)
    diagonal(2, False)
    share(2)
    home(3)
    diagonal(1, False)
    share(1)
    home(2)
    diagonal(0, False)
    share(0)
    home(1)

    for i, (a, b) in enumerate(PLANE):
        slot = lax.rem(x + a, 4) * 4 + lax.rem(y + b, 4)
        for h in range(2):
            span = pl.ds(pl.multiple_of(slot * half, 16), half)
            kv_out[i, 0, h * half:(h + 1) * half] = dk[h, span].astype(BF16)
            kv_out[i, 1, h * half:(h + 1) * half] = dv[h, span].astype(BF16)
        send(kv_out.at[i], kv_in.at[i], kv_recv.at[i], at_plane(a, b))
    home(0)

    totals = []
    for h in range(2):
        totals.append(dq[0, h, my_qslot])
    for r in (0, 1, 2, 3):
        for o in ROUNDS[r]:
            if o != 0:
                arrived(dq_in.at[o + 7], dq_recv.at[o + 7])
                for h in range(2):
                    totals[h] = totals[h] + dq_in[o + 7, h * half:(h + 1) * half].astype(F32)
    for h in range(2):
        gq_ref[h * half:(h + 1) * half] = (totals[h] * scale).astype(BF16)

    for i in range(15):
        arrived(kv_in.at[i], kv_recv.at[i])
    for h in range(2):
        span = pl.ds(pl.multiple_of(my_kslot * half, 16), half)
        rowspan = slice(h * half, (h + 1) * half)
        sk, sv = dk[h, span], dv[h, span]
        for i in range(15):
            sk = sk + kv_in[i, 0, rowspan].astype(F32)
            sv = sv + kv_in[i, 1, rowspan].astype(F32)
        gk_ref[rowspan] = (sk * scale).astype(BF16)
        gv_ref[rowspan] = sv.astype(BF16)

    for cp in sends:
        cp.wait_send()

    @pl.when(jnp.logical_not(to_self))
    def _():
        m_copy.wait_send()

    @pl.when(collects)
    def _():
        for cp in mb_copies:
            cp.wait_send()


def shards(queries, key_vectors, value_vectors, outputs, out_grad, logsumexp, positions):
    shard, width = queries.shape
    half = shard // 2
    vmem = pl.BlockSpec(memory_space=pltpu.VMEM)
    dma = pltpu.SemaphoreType.DMA
    return pl.pallas_call(
        functools.partial(kernel, half),
        name="attention_backward",
        out_shape=[jax.ShapeDtypeStruct((shard, width), BF16)] * 3,
        in_specs=[vmem] * 7,
        out_specs=[vmem] * 3,
        scratch_shapes=[
            pltpu.VMEM((4, 8, 2 * shard + 32, width), BF16),
            pltpu.VMEM((16, 2 * shard, width), BF16),
            pltpu.VMEM((8, 128), F32),
            pltpu.VMEM((1, 128), F32),
            pltpu.VMEM((16, 1, 128), F32),
            pltpu.VMEM((2, 16 * half, 128), F32),
            pltpu.VMEM((4, 8, 8 * half), F32),
            pltpu.VMEM((4, 2, 8, half, width), F32),
            pltpu.VMEM((2, 16 * half, width), F32),
            pltpu.VMEM((2, 16 * half, width), F32),
            pltpu.VMEM((4, 4, shard, width), BF16),
            pltpu.VMEM((4, 4, shard, width), BF16),
            pltpu.VMEM((4, 4, shard, width), BF16),
            pltpu.VMEM((16, shard, width), BF16),
            pltpu.VMEM((15, 2, shard, width), BF16),
            pltpu.VMEM((15, 2, shard, width), BF16),
            dma((128,)),
            dma((16,)),
            dma((16,)),
            dma((15,)),
            dma((16,)),
            dma((1,)),
            dma((4,)),
            dma((16,)),
            dma((15,)),
        ],
        compiler_params=pltpu.CompilerParams(
            collective_id=0, has_side_effects=True, vmem_limit_bytes=48 * 2 ** 20
        ),
    )(
        queries, key_vectors, value_vectors, outputs, out_grad,
        logsumexp.reshape(1, shard), positions.reshape(1, shard),
    )


def solution(mesh):
    in_specs = (
        P(("row", "col"), None),
        P(("col", "row"), None),
        P(("col", "row"), None),
        P(("row", "col"), None),
        P(("row", "col"), None),
        P(("row", "col")),
        P(("row", "col")),
    )
    out_specs = (P(("row", "col"), None), P(("col", "row"), None), P(("col", "row"), None))
    return jax.shard_map(shards, mesh=mesh, in_specs=in_specs, out_specs=out_specs, check_vma=False)
```

time: 1140 us -> 74.6 us (0.07)
  the two profiles are of different devices: /device:TPU:16 before, /device:TPU:1 now
where the time goes in v1:
time: 74.6 us; the launch traced here: 74.2 us
  Pallas kernels  67.3 us (90%)
  local copies, waits for them, and re-layouts  6.17 us (8%)
    pallas_call x1, Pallas kernels, shards(): pl.pallas_call(functools.partial(kernel, half), name='attention_backward'...  67.3 us
    unnamed x17, local copies, waits for them, and re-layouts  6.17 us

profile of v1, /device:TPU:1, one launch (start us, length us, event | category | flops | bytes accessed | tf_op | source)
XLA Modules:
  0.0 74.2 jit_solution(3401142238719088370)
XLA Ops:
  0.6 0.0 copy-start.5
  0.6 0.0 copy-start.6
  0.7 0.6 copy-done.5
  1.3 0.0 copy-done.6
  1.3 0.0 copy-start
  1.3 0.7 copy-done
  2.0 0.0 copy-start.1
  2.0 0.7 copy-done.1
  2.8 0.0 copy-start.2
  2.8 0.7 copy-done.2
  3.5 0.0 copy-start.3
  3.5 0.7 copy-done.3
  4.3 0.0 copy-start.4
  4.3 0.7 copy-done.4
  5.0 67.3 %attention_backward.1 = (bf16[96,128]{1,0:T(8,128)(2,1)S(1)}, bf16[96,128]{1,0:T(8,128)(2,1)S(1)}, bf16[96,128]{1,0:T(8,128)(2,1)S(1)}) custom-call(bf16[96,128]{1,0:T(8,128)(2,1)S(1)} %copy-done, bf16[96,128]{1,0:T(8,128)(2,1)S(1)} %copy-done.1, bf16[96,128]{1,0:T(8,128)(2,1)S(1)} %copy-done.2, bf16[96,128]{1,0:T(8,128)(2,1)S(1)} %copy-done.3, ...), custom_call_target="tpu_custom_call" | custom-call | tf_op jit(solution)/shard_map/attention_backward/pallas_call | solution.py:372
  72.3 0.6 copy.13
  73.0 0.6 copy.14
  73.6 0.6 copy.15
Async XLA Ops:
  0.6 0.7 copy-start.5
  0.6 0.7 copy-start.6
  1.3 0.7 copy-start
  2.0 0.7 copy-start.1
  2.8 0.7 copy-start.2
  3.5 0.7 copy-start.3
  4.3 0.7 copy-start.4

commit v2 on v1

--- a/solution.py
+++ b/solution.py
@@ -17,6 +17,9 @@
 
 ROUNDS = ((0, -1, 1, 2), (-2, 3, -3, 4), (-4, 5, -5, 6), (-6, 7, -7, 8))
 ROUND_OF = {o: r for r, offs in enumerate(ROUNDS) for o in offs}
+HAND_ON = {8: 7, -7: -6, 6: 5, -5: -4, 4: 3, -3: -2, 2: 1}
+TAKES = {b: a for a, b in HAND_ON.items()}
+FINAL = tuple(o for offs in ROUNDS for o in offs if o != 0 and o not in HAND_ON)
 PLANE = [(a, b) for a in range(4) for b in range(4) if (a, b) != (0, 0)]
 
 
@@ -29,13 +32,13 @@
 
 
 def kernel(
-    half, q_ref, k_ref, v_ref, o_ref, do_ref, lse_ref, pos_ref,
+    half, q_hbm, k_hbm, v_hbm, o_hbm, do_hbm, lse_hbm, pos_hbm,
     gq_ref, gk_ref, gv_ref,
-    qbuf, kbuf, rowbuf, mrow, mbuf, pk, rows, dq, dk, dv,
-    sib_out, sib_in, dq_out, dq_in, kv_out, kv_in,
-    send_sem, q_recv, qs_recv, k_recv, m_recv, mb_recv, sib_recv, dq_recv, kv_recv,
+    qbuf, kbuf, o_ref, lse_ref, pos_ref, rowbuf, mrow, mbuf, pk, rows, dq, dk, dv,
+    sib_out, sib_in, dq_out, pair_in, dq_in, kv_out, kv_in,
+    in_sem, send_sem, q_recv, qs_recv, k_recv, m_recv, mb_recv, sib_recv, pair_recv, dq_recv, kv_recv,
 ):
-    width = q_ref.shape[1]
+    width = q_hbm.shape[1]
     shard = 2 * half
     scale = width ** -0.5
     row, col = lax.axis_index("row"), lax.axis_index("col")
@@ -62,6 +65,23 @@
         xo, yo = slot // 4, slot % 4
         hz, hc = (xo // 2) * 8 + 2 * yo + z_hi, xo % 2
         return hz, hc, jnp.logical_and(hz == z, hc == core)
+
+    my_qslot = lax.rem(z, 4) * 2 + core
+    my_kslot = x * 4 + y
+    inputs = [
+        pltpu.make_async_copy(src, dst, in_sem.at[i])
+        for i, (src, dst) in enumerate((
+            (do_hbm, qbuf.at[0, my_qslot, pl.ds(shard, shard)]),
+            (o_hbm, o_ref),
+            (lse_hbm, lse_ref),
+            (pos_hbm, pos_ref),
+            (q_hbm, qbuf.at[0, my_qslot, pl.ds(0, shard)]),
+            (k_hbm, kbuf.at[my_kslot, pl.ds(0, shard)]),
+            (v_hbm, kbuf.at[my_kslot, pl.ds(shard, shard)]),
+        ))
+    ]
+    for cp in inputs:
+        cp.start()
 
     barrier = pltpu.get_barrier_semaphore()
     for o in range(1, 16):
@@ -94,13 +114,9 @@
             device_id=sibling, device_id_type=MESH,
         ).wait_recv()
 
-    my_qslot = lax.rem(z, 4) * 2 + core
-    my_kslot = x * 4 + y
-    qbuf[0, my_qslot, 0:shard] = q_ref[...]
-    qbuf[0, my_qslot, shard:2 * shard] = do_ref[...]
-    kbuf[my_kslot, 0:shard] = k_ref[...]
-    kbuf[my_kslot, shard:2 * shard] = v_ref[...]
-    prod = do_ref[...].astype(F32) * o_ref[...].astype(F32)
+    for cp in inputs:
+        cp.wait()
+    prod = qbuf[0, my_qslot, shard:2 * shard].astype(F32) * o_ref[...].astype(F32)
     rowbuf[...] = jnp.zeros_like(rowbuf)
     rowbuf[0:1, 0:shard] = lse_ref[...] * LOG2E
     rowbuf[1:2, 0:shard] = jnp.sum(prod.T, axis=0, keepdims=True)
@@ -116,9 +132,7 @@
     )
     hi = full.astype(BF16).astype(F32)
     mid = (full - hi).astype(BF16).astype(F32)
-    low = full - hi - mid
-    parts = jnp.concatenate([hi, mid, low, jnp.zeros_like(hi)], axis=0)
-    qbuf[0, my_qslot, 2 * shard:2 * shard + 32] = parts.astype(BF16)
+    qbuf[0, my_qslot, 2 * shard:2 * shard + 16] = jnp.concatenate([hi, mid], axis=0).astype(BF16)
 
     pl.semaphore_wait(barrier, 31 + jnp.where(to_self, 0, 1))
 
@@ -128,22 +142,42 @@
     def sslot(o):
         return lax.rem(z + o + 16, 4) * 2 + other
 
-    def relay(o):
-        src = qbuf.at[ROUND_OF[o], qslot(o)]
-        for sign in ((1, -1) if o == 0 else ((1,) if o < 0 else (-1,))):
-            for d in (2, 1):
-                there = o - sign * d
-                if there in ROUND_OF and abs(there) <= 8:
-                    send(src, qbuf.at[ROUND_OF[there], qslot(o)], q_recv.at[there + 7], at_z(sign * d))
+    chunks = (pl.ds(0, shard), pl.ds(shard, shard + 16))
+
+    def directions(o):
+        return (1, -1) if o == 0 else ((1,) if o < 0 else (-1,))
+
+    def relay(o, c):
+        for sign in directions(o):
+            there = o - sign * 2
+            if there in ROUND_OF:
+                send(
+                    qbuf.at[ROUND_OF[o], qslot(o), chunks[c]],
+                    qbuf.at[ROUND_OF[there], qslot(o), chunks[c]],
+                    q_recv.at[c, there + 7], at_z(sign * 2),
+                )
+
+    def deliver(o):
+        for sign in directions(o):
+            there = o - sign
+            send(
+                qbuf.at[ROUND_OF[o], qslot(o)], qbuf.at[ROUND_OF[there], qslot(o)],
+                q_recv.at[1, there + 7], at_z(sign),
+            )
 
     def to_sibling(o):
         ref = qbuf.at[ROUND_OF[o], qslot(o)]
         send(ref, ref, qs_recv.at[o + 7], sibling)
 
-    def take(o):
-        arrived(qbuf.at[ROUND_OF[o], qslot(o)], q_recv.at[o + 7])
-
-    relay(0)
+    def take(o, c):
+        arrived(qbuf.at[ROUND_OF[o], qslot(o), chunks[c]], q_recv.at[c, o + 7])
+
+    def take_whole(o):
+        arrived(qbuf.at[ROUND_OF[o], qslot(o)], q_recv.at[1, o + 7])
+
+    relay(0, 0)
+    relay(0, 1)
+    deliver(0)
     to_sibling(0)
     for i, (a, b) in enumerate(PLANE):
         ref = kbuf.at[my_kslot]
@@ -168,8 +202,8 @@
         tiles = []
         pieces = []
         for s in range(8):
-            raw = qbuf[r, s, 2 * shard:2 * shard + 32].astype(F32)
-            pieces.append(raw[0:8] + raw[8:16] + raw[16:24])
+            raw = qbuf[r, s, 2 * shard:2 * shard + 16].astype(F32)
+            pieces.append(raw[0:8] + raw[8:16])
         for j in range(8 * half // 128):
             first, last = 128 * j // half, (128 * j + 127) // half
             tile = pieces[last]
@@ -219,9 +253,11 @@
         for kb in range(2):
             block(r, 0, 1, kb, False, kb == 0, first)
 
-    def diagonal(r, first):
+    def early_early(r):
         for kb in range(2):
             block(r, 0, 0, kb, True, kb == 0, False)
+
+    def late_late(r, first):
         for kb in range(2):
             block(r, 1, 1, kb, True, False, first)
 
@@ -231,15 +267,62 @@
         unpack(r)
 
     def stage(k):
-        for o in (-2 * k, 2 * k):
-            if o in ROUND_OF:
-                take(o)
+        far = [o for o in (-2 * k, 2 * k) if o in ROUND_OF]
+        for c in range(2):
+            for o in far:
+                take(o, c)
                 if k < 4:
-                    relay(o)
-                to_sibling(o)
+                    relay(o, c)
+        for o in far:
+            if k < 4:
+                deliver(o)
+            to_sibling(o)
         for o in (-2 * k + 1, 2 * k - 1):
-            take(o)
+            take_whole(o)
             to_sibling(o)
+
+    def share(r):
+        for i, o in enumerate(ROUNDS[r]):
+            sib_out[r, i, 0:half] = dq[r, 0, sslot(o)].astype(BF16)
+            sib_out[r, i, half:shard] = dq[r, 1, sslot(o)].astype(BF16)
+        send(sib_out.at[r], sib_in.at[r], sib_recv.at[r], sibling)
+
+    def home_far(r):
+        arrived(sib_in.at[r], sib_recv.at[r])
+        for i, o in enumerate(ROUNDS[r]):
+            if o in HAND_ON or o == -1:
+                for h in range(2):
+                    span = slice(h * half, (h + 1) * half)
+                    dq_out[r, i, span] = (dq[r, h, qslot(o)] + sib_in[r, i, span].astype(F32)).astype(BF16)
+                if o == -1:
+                    send(dq_out.at[r, i], dq_in.at[FINAL.index(o)], dq_recv.at[FINAL.index(o)], at_z(o))
+                else:
+                    there = HAND_ON[o]
+                    j = ROUNDS[r].index(there)
+                    send(dq_out.at[r, i], pair_in.at[r, j], pair_recv.at[r, j], at_z(o - there))
+
+    def home_near(r):
+        for i, o in enumerate(ROUNDS[r]):
+            if o in TAKES or o == 0:
+                if o != 0:
+                    arrived(pair_in.at[r, i], pair_recv.at[r, i])
+                for h in range(2):
+                    span = slice(h * half, (h + 1) * half)
+                    total = dq[r, h, qslot(o)] + sib_in[r, i, span].astype(F32)
+                    if o == 0:
+                        dq[r, h, qslot(o)] = total
+                    else:
+                        dq_out[r, i, span] = (total + pair_in[r, i, span].astype(F32)).astype(BF16)
+                if o != 0:
+                    send(dq_out.at[r, i], dq_in.at[FINAL.index(o)], dq_recv.at[FINAL.index(o)], at_z(o))
+
+    def keys_home(h):
+        for i, (a, b) in enumerate(PLANE):
+            slot = lax.rem(x + a, 4) * 4 + lax.rem(y + b, 4)
+            span = pl.ds(pl.multiple_of(slot * half, 16), half)
+            kv_out[i, h, 0] = dk[h, span].astype(BF16)
+            kv_out[i, h, 1] = dv[h, span].astype(BF16)
+            send(kv_out.at[i, h], kv_in.at[i, h], kv_recv.at[i, h], at_plane(a, b))
 
     stage(1)
     ready(0)
@@ -273,9 +356,6 @@
     stage(3)
     ready(2)
     late_early(2, False)
-    stage(4)
-    ready(3)
-    late_early(3, False)
 
     @pl.when(jnp.logical_not(collects))
     def _():
@@ -287,69 +367,50 @@
         pk[0, slot * half:(slot + 1) * half] = start + sub48
         pk[1, slot * half:(slot + 1) * half] = top - start + sub48
 
-    def share(r):
-        for i, o in enumerate(ROUNDS[r]):
-            sib_out[r, i, 0:half] = dq[r, 0, sslot(o)].astype(BF16)
-            sib_out[r, i, half:shard] = dq[r, 1, sslot(o)].astype(BF16)
-        send(sib_out.at[r], sib_in.at[r], sib_recv.at[r], sibling)
-
-    def home(r):
-        arrived(sib_in.at[r], sib_recv.at[r])
-        for i, o in enumerate(ROUNDS[r]):
-            for h in range(2):
-                span = slice(h * half, (h + 1) * half)
-                total = dq[r, h, qslot(o)] + sib_in[r, i, span].astype(F32)
-                if o == 0:
-                    dq[r, h, qslot(o)] = total
-                else:
-                    dq_out[r, i, span] = total.astype(BF16)
-            if o != 0:
-                send(dq_out.at[r, i], dq_in.at[o + 7], dq_recv.at[o + 7], at_z(o))
-
-    diagonal(3, True)
+    early_early(0)
+    late_late(0, True)
+    share(0)
+    early_early(1)
+    late_late(1, False)
+    share(1)
+    home_far(0)
+    stage(4)
+    home_near(0)
+    home_far(1)
+    ready(3)
+    late_early(3, False)
+    early_early(3)
+    late_late(3, False)
     share(3)
-    diagonal(2, False)
+    home_near(1)
+    early_early(2)
+    keys_home(0)
+    home_far(3)
+    late_late(2, False)
     share(2)
-    home(3)
-    diagonal(1, False)
-    share(1)
-    home(2)
-    diagonal(0, False)
-    share(0)
-    home(1)
-
-    for i, (a, b) in enumerate(PLANE):
-        slot = lax.rem(x + a, 4) * 4 + lax.rem(y + b, 4)
-        for h in range(2):
-            span = pl.ds(pl.multiple_of(slot * half, 16), half)
-            kv_out[i, 0, h * half:(h + 1) * half] = dk[h, span].astype(BF16)
-            kv_out[i, 1, h * half:(h + 1) * half] = dv[h, span].astype(BF16)
-        send(kv_out.at[i], kv_in.at[i], kv_recv.at[i], at_plane(a, b))
-    home(0)
-
-    totals = []
-    for h in range(2):
-        totals.append(dq[0, h, my_qslot])
-    for r in (0, 1, 2, 3):
-        for o in ROUNDS[r]:
-            if o != 0:
-                arrived(dq_in.at[o + 7], dq_recv.at[o + 7])
-                for h in range(2):
-                    totals[h] = totals[h] + dq_in[o + 7, h * half:(h + 1) * half].astype(F32)
-    for h in range(2):
-        gq_ref[h * half:(h + 1) * half] = (totals[h] * scale).astype(BF16)
-
-    for i in range(15):
-        arrived(kv_in.at[i], kv_recv.at[i])
+    keys_home(1)
+    home_near(3)
+    home_far(2)
+    home_near(2)
+
     for h in range(2):
         span = pl.ds(pl.multiple_of(my_kslot * half, 16), half)
         rowspan = slice(h * half, (h + 1) * half)
         sk, sv = dk[h, span], dv[h, span]
         for i in range(15):
-            sk = sk + kv_in[i, 0, rowspan].astype(F32)
-            sv = sv + kv_in[i, 1, rowspan].astype(F32)
+            arrived(kv_in.at[i, h], kv_recv.at[i, h])
+            sk = sk + kv_in[i, h, 0].astype(F32)
+            sv = sv + kv_in[i, h, 1].astype(F32)
         gk_ref[rowspan] = (sk * scale).astype(BF16)
         gv_ref[rowspan] = sv.astype(BF16)
+
+    totals = [dq[0, h, my_qslot] for h in range(2)]
+    for i in range(len(FINAL)):
+        arrived(dq_in.at[i], dq_recv.at[i])
+        for h in range(2):
+            totals[h] = totals[h] + dq_in[i, h * half:(h + 1) * half].astype(F32)
+    for h in range(2):
+        gq_ref[h * half:(h + 1) * half] = (totals[h] * scale).astype(BF16)
 
     for cp in sends:
         cp.wait_send()
@@ -373,11 +434,14 @@
         functools.partial(kernel, half),
         name="attention_backward",
         out_shape=[jax.ShapeDtypeStruct((shard, width), BF16)] * 3,
-        in_specs=[vmem] * 7,
+        in_specs=[pl.BlockSpec(memory_space=pltpu.HBM)] * 7,
         out_specs=[vmem] * 3,
         scratch_shapes=[
-            pltpu.VMEM((4, 8, 2 * shard + 32, width), BF16),
+            pltpu.VMEM((4, 8, 2 * shard + 16, width), BF16),
             pltpu.VMEM((16, 2 * shard, width), BF16),
+            pltpu.VMEM((shard, width), BF16),
+            pltpu.VMEM((1, shard), F32),
+            pltpu.VMEM((1, shard), jnp.int32),
             pltpu.VMEM((8, 128), F32),
             pltpu.VMEM((1, 128), F32),
             pltpu.VMEM((16, 1, 128), F32),
@@ -389,18 +453,21 @@
             pltpu.VMEM((4, 4, shard, width), BF16),
             pltpu.VMEM((4, 4, shard, width), BF16),
             pltpu.VMEM((4, 4, shard, width), BF16),
-            pltpu.VMEM((16, shard, width), BF16),
-            pltpu.VMEM((15, 2, shard, width), BF16),
-            pltpu.VMEM((15, 2, shard, width), BF16),
-            dma((128,)),
-            dma((16,)),
+            pltpu.VMEM((4, 4, shard, width), BF16),
+            pltpu.VMEM((len(FINAL), shard, width), BF16),
+            pltpu.VMEM((15, 2, 2, half, width), BF16),
+            pltpu.VMEM((15, 2, 2, half, width), BF16),
+            dma((7,)),
+            dma((160,)),
+            dma((2, 16)),
             dma((16,)),
             dma((15,)),
             dma((16,)),
             dma((1,)),
             dma((4,)),
-            dma((16,)),
-            dma((15,)),
+            dma((4, 4)),
+            dma((len(FINAL),)),
+            dma((15, 2)),
         ],
         compiler_params=pltpu.CompilerParams(
             collective_id=0, has_side_effects=True, vmem_limit_bytes=48 * 2 ** 20

time: 74.6 us -> 70.7 us (0.948); the launches traced: 74.2 us -> 69.4 us
  Pallas kernels: 67.3 us -> 62.6 us
    pallas_call x1, Pallas kernels: 67.3 us -> 62.6 us  [shards(): pl.pallas_call(functools.partial(kernel, half), name='attention_backward'...]
where the time goes in v2:
time: 70.7 us; the launch traced here: 69.4 us
  Pallas kernels  62.6 us (89%)
  local copies, waits for them, and re-layouts  6.17 us (9%)
    pallas_call x1, Pallas kernels, shards(): pl.pallas_call(functools.partial(kernel, half), name='attention_backward'...  62.6 us
    unnamed x17, local copies, waits for them, and re-layouts  6.17 us

profile of v2, /device:TPU:1, one launch (start us, length us, event | category | flops | bytes accessed | tf_op | source)
XLA Modules:
  0.0 69.4 jit_solution(15222254242547481036)
XLA Ops:
  0.6 0.0 copy-start.5
  0.6 0.0 copy-start.6
  0.7 0.6 copy-done.5
  1.3 0.0 copy-done.6
  1.3 0.0 copy-start
  1.3 0.7 %copy-done = bf16[96,128]{1,0:T(8,128)(2,1)S(1)} copy-done((bf16[96,128]{1,0:T(8,128)(2,1)S(1)}, bf16[96,128]{1,0:T(8,128)(2,1)}, u32[]{:S(2)}) %copy-start) | copy-done | bytes 24600
  2.0 0.0 copy-start.1
  2.0 0.7 %copy-done.1 = bf16[96,128]{1,0:T(8,128)(2,1)S(1)} copy-done((bf16[96,128]{1,0:T(8,128)(2,1)S(1)}, bf16[96,128]{1,0:T(8,128)(2,1)}, u32[]{:S(2)}) %copy-start.1) | copy-done | bytes 24600
  2.8 0.0 copy-start.2
  2.8 0.7 %copy-done.2 = bf16[96,128]{1,0:T(8,128)(2,1)S(1)} copy-done((bf16[96,128]{1,0:T(8,128)(2,1)S(1)}, bf16[96,128]{1,0:T(8,128)(2,1)}, u32[]{:S(2)}) %copy-start.2) | copy-done | bytes 24600
  3.5 0.0 copy-start.3
  3.5 0.7 %copy-done.3 = bf16[96,128]{1,0:T(8,128)(2,1)S(1)} copy-done((bf16[96,128]{1,0:T(8,128)(2,1)S(1)}, bf16[96,128]{1,0:T(8,128)(2,1)}, u32[]{:S(2)}) %copy-start.3) | copy-done | bytes 24600
  4.3 0.0 copy-start.4
  4.3 0.7 %copy-done.4 = bf16[96,128]{1,0:T(8,128)(2,1)S(1)} copy-done((bf16[96,128]{1,0:T(8,128)(2,1)S(1)}, bf16[96,128]{1,0:T(8,128)(2,1)}, u32[]{:S(2)}) %copy-start.4) | copy-done | bytes 24600
  5.0 62.6 %attention_backward.1 = (bf16[96,128]{1,0:T(8,128)(2,1)S(1)}, bf16[96,128]{1,0:T(8,128)(2,1)S(1)}, bf16[96,128]{1,0:T(8,128)(2,1)S(1)}) custom-call(bf16[96,128]{1,0:T(8,128)(2,1)S(1)} %copy-done, bf16[96,128]{1,0:T(8,128)(2,1)S(1)} %copy-done.1, bf16[96,128]{1,0:T(8,128)(2,1)S(1)} %copy-done.2, bf16[96,128]{1,0:T(8,128)(2,1)S(1)} %copy-done.3, ...), custom_call_target="tpu_custom_call" | custom-call | tf_op jit(solution)/shard_map/attention_backward/pallas_call | solution.py:433
  67.6 0.6 copy.13
  68.2 0.6 copy.14
  68.8 0.6 copy.15
Async XLA Ops:
  0.6 0.7 copy-start.5
  0.6 0.7 copy-start.6
  1.3 0.7 %copy-start = (bf16[96,128]{1,0:T(8,128)(2,1)S(1)}, bf16[96,128]{1,0:T(8,128)(2,1)}, u32[]{:S(2)}) copy-start(bf16[96,128]{1,0:T(8,128)(2,1)} %q_hbm.1) | copy-start | bytes 73732
  2.0 0.7 %copy-start.1 = (bf16[96,128]{1,0:T(8,128)(2,1)S(1)}, bf16[96,128]{1,0:T(8,128)(2,1)}, u32[]{:S(2)}) copy-start(bf16[96,128]{1,0:T(8,128)(2,1)} %k_hbm.1) | copy-start | bytes 73732
  2.8 0.7 %copy-start.2 = (bf16[96,128]{1,0:T(8,128)(2,1)S(1)}, bf16[96,128]{1,0:T(8,128)(2,1)}, u32[]{:S(2)}) copy-start(bf16[96,128]{1,0:T(8,128)(2,1)} %v_hbm.1) | copy-start | bytes 73732
  3.5 0.7 %copy-start.3 = (bf16[96,128]{1,0:T(8,128)(2,1)S(1)}, bf16[96,128]{1,0:T(8,128)(2,1)}, u32[]{:S(2)}) copy-start(bf16[96,128]{1,0:T(8,128)(2,1)} %o_hbm.1) | copy-start | bytes 73732
  4.3 0.7 %copy-start.4 = (bf16[96,128]{1,0:T(8,128)(2,1)S(1)}, bf16[96,128]{1,0:T(8,128)(2,1)}, u32[]{:S(2)}) copy-start(bf16[96,128]{1,0:T(8,128)(2,1)} %do_hbm.1) | copy-start | bytes 73732

commit v3 on v2

--- a/solution.py
+++ b/solution.py
@@ -17,10 +17,10 @@
 
 ROUNDS = ((0, -1, 1, 2), (-2, 3, -3, 4), (-4, 5, -5, 6), (-6, 7, -7, 8))
 ROUND_OF = {o: r for r, offs in enumerate(ROUNDS) for o in offs}
-HAND_ON = {8: 7, -7: -6, 6: 5, -5: -4, 4: 3, -3: -2, 2: 1}
+HAND_ON = {8: 6, 7: 5, -7: -5, -6: -4, 4: 3, -3: -2, 2: 1}
 TAKES = {b: a for a, b in HAND_ON.items()}
 FINAL = tuple(o for offs in ROUNDS for o in offs if o != 0 and o not in HAND_ON)
-PLANE = [(a, b) for a in range(4) for b in range(4) if (a, b) != (0, 0)]
+PLANE = [(a, b) for b in (0, 1, 3, 2) for a in (1, 3, 2, 0) if (a, b) != (0, 0)]
 
 
 def dot(a, b, dims):
@@ -34,9 +34,9 @@
 def kernel(
     half, q_hbm, k_hbm, v_hbm, o_hbm, do_hbm, lse_hbm, pos_hbm,
     gq_ref, gk_ref, gv_ref,
-    qbuf, kbuf, o_ref, lse_ref, pos_ref, rowbuf, mrow, mbuf, pk, rows, dq, dk, dv,
+    qbuf, kbuf, o_ref, lse_ref, pos_ref, rowbuf, mrow, mstage, mbuf, pk, rows, dq, dk, dv,
     sib_out, sib_in, dq_out, pair_in, dq_in, kv_out, kv_in,
-    in_sem, send_sem, q_recv, qs_recv, k_recv, m_recv, mb_recv, sib_recv, pair_recv, dq_recv, kv_recv,
+    in_sem, send_sem, q_recv, qs_recv, k_recv, ms_recv, m_recv, mb_recv, sib_recv, pair_recv, dq_recv, kv_recv,
 ):
     width = q_hbm.shape[1]
     shard = 2 * half
@@ -84,19 +84,11 @@
         cp.start()
 
     barrier = pltpu.get_barrier_semaphore()
-    for o in range(1, 16):
-        pl.semaphore_signal(barrier, inc=1, device_id=at_z(o), device_id_type=MESH)
-    for a, b in PLANE:
-        pl.semaphore_signal(barrier, inc=1, device_id=at_plane(a, b), device_id_type=MESH)
-    pl.semaphore_signal(barrier, inc=1, device_id=sibling, device_id_type=MESH)
-    for slot in range(16):
-        hz, hc, mine = holder(slot)
-
-        @pl.when(jnp.logical_and(collects, jnp.logical_not(mine)))
-        def _():
-            pl.semaphore_signal(
-                barrier, inc=1, device_id=device(x, y, hz, hc), device_id_type=MESH
-            )
+    greeted = [at_plane(a, b) for a, b in PLANE] + [sibling]
+    for o in (-4, -3, -2, -1, 1, 2, 3, 4):
+        greeted += [at_z(o), device(x, y, lax.rem(z + o + 16, 16), other)]
+    for target in greeted:
+        pl.semaphore_signal(barrier, inc=1, device_id=target, device_id_type=MESH)
 
     sends = []
 
@@ -134,7 +126,7 @@
     mid = (full - hi).astype(BF16).astype(F32)
     qbuf[0, my_qslot, 2 * shard:2 * shard + 16] = jnp.concatenate([hi, mid], axis=0).astype(BF16)
 
-    pl.semaphore_wait(barrier, 31 + jnp.where(to_self, 0, 1))
+    pl.semaphore_wait(barrier, len(greeted))
 
     def qslot(o):
         return lax.rem(z + o + 16, 4) * 2 + core
@@ -175,22 +167,58 @@
     def take_whole(o):
         arrived(qbuf.at[ROUND_OF[o], qslot(o)], q_recv.at[1, o + 7])
 
+    def keys_out(first, last):
+        for i in range(first, last):
+            ref = kbuf.at[my_kslot]
+            send(ref, ref, k_recv.at[i], at_plane(*PLANE[i]))
+
     relay(0, 0)
     relay(0, 1)
+    to_sibling(0)
     deliver(0)
-    to_sibling(0)
-    for i, (a, b) in enumerate(PLANE):
-        ref = kbuf.at[my_kslot]
-        send(ref, ref, k_recv.at[i], at_plane(a, b))
-
-    m_copy = pltpu.make_async_remote_copy(
-        src_ref=mrow, dst_ref=mbuf.at[my_mslot], send_sem=send_sem.at[send_sem.shape[0] - 1],
+    keys_out(0, 15)
+
+    ahead = lax.rem(to_z - z + 16, 16)
+    ahead = jnp.where(ahead > 8, ahead - 16, ahead)
+    last = send_sem.shape[0] - 1
+
+    m_direct = pltpu.make_async_remote_copy(
+        src_ref=mrow, dst_ref=mbuf.at[my_mslot], send_sem=send_sem.at[last],
         recv_sem=m_recv.at[my_mslot], device_id=device(x, y, to_z, to_core), device_id_type=MESH,
     )
-
-    @pl.when(jnp.logical_not(to_self))
+    m_first = {
+        sign: pltpu.make_async_remote_copy(
+            src_ref=mrow, dst_ref=mstage.at[2 * j + core], send_sem=send_sem.at[last],
+            recv_sem=ms_recv.at[2 * j + core],
+            device_id=device(x, y, lax.rem(z + 4 * sign + 16, 16), to_core), device_id_type=MESH,
+        )
+        for j, sign in enumerate((1, -1))
+    }
+    m_onward = []
+    for j, sign in enumerate((1, -1)):
+        for hc in range(2):
+            hz = lax.rem(z - 4 * sign + 16, 16)
+            far = lax.rem(to_z - hz + 16, 16)
+            far = jnp.where(far > 8, far - 16, far)
+            mslot = (hz // 8 * 2 + hc) * 4 + lax.rem(hz, 8) // 2
+            m_onward.append((
+                jnp.logical_and(core == to_core, far * sign > 4),
+                pltpu.make_async_remote_copy(
+                    src_ref=mstage.at[2 * j + hc], dst_ref=mbuf.at[mslot], send_sem=send_sem.at[last - 16 - 2 * j - hc],
+                    recv_sem=m_recv.at[mslot], device_id=device(x, y, to_z, to_core), device_id_type=MESH,
+                ),
+            ))
+    m_near = jnp.logical_and(jnp.logical_not(to_self), jnp.abs(ahead) <= 4)
+
+    @pl.when(m_near)
     def _():
-        m_copy.start()
+        m_direct.start()
+
+    for sign in (1, -1):
+
+        @pl.when(ahead * sign > 4)
+        def _():
+            m_first[sign].start()
 
     @pl.when(to_self)
     def _():
@@ -290,16 +318,17 @@
     def home_far(r):
         arrived(sib_in.at[r], sib_recv.at[r])
         for i, o in enumerate(ROUNDS[r]):
-            if o in HAND_ON or o == -1:
+            if o in HAND_ON or (o != 0 and o not in TAKES):
                 for h in range(2):
                     span = slice(h * half, (h + 1) * half)
                     dq_out[r, i, span] = (dq[r, h, qslot(o)] + sib_in[r, i, span].astype(F32)).astype(BF16)
-                if o == -1:
+                if o not in HAND_ON:
                     send(dq_out.at[r, i], dq_in.at[FINAL.index(o)], dq_recv.at[FINAL.index(o)], at_z(o))
                 else:
                     there = HAND_ON[o]
-                    j = ROUNDS[r].index(there)
-                    send(dq_out.at[r, i], pair_in.at[r, j], pair_recv.at[r, j], at_z(o - there))
+                    rt = ROUND_OF[there]
+                    j = ROUNDS[rt].index(there)
+                    send(dq_out.at[r, i], pair_in.at[rt, j], pair_recv.at[rt, j], at_z(o - there))
 
     def home_near(r):
         for i, o in enumerate(ROUNDS[r]):
@@ -325,11 +354,17 @@
             send(kv_out.at[i, h], kv_in.at[i, h], kv_recv.at[i, h], at_plane(a, b))
 
     stage(1)
+
+    for i, (used, cp) in enumerate(m_onward):
+
+        @pl.when(used)
+        def _():
+            arrived(mstage.at[i], ms_recv.at[i])
+            cp.start()
+
     ready(0)
-    for i, (a, b) in enumerate(PLANE):
-        arrived(kbuf.at[lax.rem(x - a + 4, 4) * 4 + lax.rem(y - b + 4, 4)], k_recv.at[i])
-    late_early(0, True)
     stage(2)
+    ready(1)
 
     for slot in range(16):
         hz, hc, mine = holder(slot)
@@ -351,7 +386,9 @@
         for cp in mb_copies:
             cp.start()
 
-    ready(1)
+    for i, (a, b) in enumerate(PLANE):
+        arrived(kbuf.at[lax.rem(x - a + 4, 4) * 4 + lax.rem(y - b + 4, 4)], k_recv.at[i])
+    late_early(0, True)
     late_early(1, False)
     stage(3)
     ready(2)
@@ -389,8 +426,7 @@
     late_late(2, False)
     share(2)
     keys_home(1)
-    home_near(3)
-    home_far(2)
+    arrived(sib_in.at[2], sib_recv.at[2])
     home_near(2)
 
     for h in range(2):
@@ -415,9 +451,21 @@
     for cp in sends:
         cp.wait_send()
 
-    @pl.when(jnp.logical_not(to_self))
+    @pl.when(m_near)
     def _():
-        m_copy.wait_send()
+        m_direct.wait_send()
+
+    for sign in (1, -1):
+
+        @pl.when(ahead * sign > 4)
+        def _():
+            m_first[sign].wait_send()
+
+    for used, cp in m_onward:
+
+        @pl.when(used)
+        def _():
+            cp.wait_send()
 
     @pl.when(collects)
     def _():
@@ -444,6 +492,7 @@
             pltpu.VMEM((1, shard), jnp.int32),
             pltpu.VMEM((8, 128), F32),
             pltpu.VMEM((1, 128), F32),
+            pltpu.VMEM((4, 1, 128), F32),
             pltpu.VMEM((16, 1, 128), F32),
             pltpu.VMEM((2, 16 * half, 128), F32),
             pltpu.VMEM((4, 8, 8 * half), F32),
@@ -462,6 +511,7 @@
             dma((2, 16)),
             dma((16,)),
             dma((15,)),
+            dma((4,)),
             dma((16,)),
             dma((1,)),
             dma((4,)),
@@ -470,7 +520,7 @@
             dma((15, 2)),
         ],
         compiler_params=pltpu.CompilerParams(
-            collective_id=0, has_side_effects=True, vmem_limit_bytes=48 * 2 ** 20
+            collective_id=0, has_side_effects=True, vmem_limit_bytes=60 * 2 ** 20
         ),
     )(
         queries, key_vectors, value_vectors, outputs, out_grad,

time: 70.7 us -> 62.8 us (0.89)
  the two profiles are of different devices: /device:TPU:1 before, /device:TPU:8 now
where the time goes in v3:
time: 62.8 us; the launch traced here: 62.5 us
  Pallas kernels  59.1 us (94%)
  local copies, waits for them, and re-layouts  2.71 us (4%)
  between operations  0.65 us (1%)
    pallas_call x1, Pallas kernels, shards(): pl.pallas_call(functools.partial(kernel, half), name='attention_backward'...  59.1 us
    unnamed x7, local copies, waits for them, and re-layouts  2.71 us

profile of v3, /device:TPU:8, one launch (start us, length us, event | category | flops | bytes accessed | tf_op | source)
XLA Modules:
  0.0 62.5 jit_solution(4190798548159743147)
XLA Ops:
  0.6 59.1 %attention_backward.1 = (bf16[96,128]{1,0:T(8,128)(2,1)}, bf16[96,128]{1,0:T(8,128)(2,1)}, bf16[96,128]{1,0:T(8,128)(2,1)}) custom-call(bf16[96,128]{1,0:T(8,128)(2,1)} %q_hbm.1, bf16[96,128]{1,0:T(8,128)(2,1)} %k_hbm.1, bf16[96,128]{1,0:T(8,128)(2,1)} %v_hbm.1, bf16[96,128]{1,0:T(8,128)(2,1)} %o_hbm.1, bf16[96,128]{1,0:T(8,128)(2,1)} %do_hbm.1, ...), custom_call_target="tpu_custom_call" | custom-call | tf_op jit(solution)/shard_map/attention_backward/pallas_call | solution.py:481
  59.8 0.0 copy-start.1
  59.8 1.4 %copy.13 = bf16[96,128]{1,0:T(8,128)(2,1)} copy(bf16[96,128]{1,0:T(8,128)(2,1)} %get-tuple-element.6) | data formatting | bytes 49152
  61.2 0.0 copy-done.1
  61.2 0.0 copy-start
  61.2 0.6 copy.14
  61.8 0.1 copy-done
  61.9 0.6 copy.15
Async XLA Ops:
  59.8 1.4 %copy-start.1 = (bf16[96,128]{1,0:T(8,128)(2,1)S(1)}, bf16[96,128]{1,0:T(8,128)(2,1)}, u32[]{:S(2)}) copy-start(bf16[96,128]{1,0:T(8,128)(2,1)} %get-tuple-element.7) | copy-start | bytes 73732
  61.2 0.7 %copy-start = (bf16[96,128]{1,0:T(8,128)(2,1)S(1)}, bf16[96,128]{1,0:T(8,128)(2,1)}, u32[]{:S(2)}) copy-start(bf16[96,128]{1,0:T(8,128)(2,1)} %get-tuple-element.8) | copy-start | bytes 73732

commit v4 on v3

--- a/solution.py
+++ b/solution.py
@@ -20,7 +20,15 @@
 HAND_ON = {8: 6, 7: 5, -7: -5, -6: -4, 4: 3, -3: -2, 2: 1}
 TAKES = {b: a for a, b in HAND_ON.items()}
 FINAL = tuple(o for offs in ROUNDS for o in offs if o != 0 and o not in HAND_ON)
-PLANE = [(a, b) for b in (0, 1, 3, 2) for a in (1, 3, 2, 0) if (a, b) != (0, 0)]
+PLANE = (
+    (2, 2), (3, 2), (2, 1), (0, 2), (1, 2), (3, 1), (2, 3), (0, 1), (1, 1), (3, 3), (1, 3), (0, 3), (2, 0), (3, 0), (1, 0),
+)
+PAIRS = tuple(sorted(set(HAND_ON.values())))
+CHUNK, DELIVER, SIBLING, KEYS, SHARE, HOME, KEYS_HOME, M_FIRST, M_LAST, M_ONWARD = 0, 2, 3, 4, 5, 6, 7, 8, 9, 10
+
+
+def q_index(o, c):
+    return (o + 7) // 2 if o % 2 else 8 + (o // 2 + (3 if o < 0 else 2)) * 2 + c
 
 
 def dot(a, b, dims):
@@ -33,8 +41,8 @@
 
 def kernel(
     half, q_hbm, k_hbm, v_hbm, o_hbm, do_hbm, lse_hbm, pos_hbm,
-    gq_ref, gk_ref, gv_ref,
-    qbuf, kbuf, o_ref, lse_ref, pos_ref, rowbuf, mrow, mstage, mbuf, pk, rows, dq, dk, dv,
+    out_ref,
+    qbuf, kbuf, o_ref, lse_ref, pos_ref, rowbuf, mrow, mstage, mbuf, mwide, pk, rows, dq, dk, dv,
     sib_out, sib_in, dq_out, pair_in, dq_in, kv_out, kv_in,
     in_sem, send_sem, q_recv, qs_recv, k_recv, ms_recv, m_recv, mb_recv, sib_recv, pair_recv, dq_recv, kv_recv,
 ):
@@ -60,11 +68,6 @@
     to_self = jnp.logical_and(to_z == z, to_core == core)
     my_mslot = (z_hi * 2 + core) * 4 + z_lo // 2
     collects = jnp.logical_and(x == core * 2 + z_lo // 4, y == lax.rem(z_lo, 4))
-
-    def holder(slot):
-        xo, yo = slot // 4, slot % 4
-        hz, hc = (xo // 2) * 8 + 2 * yo + z_hi, xo % 2
-        return hz, hc, jnp.logical_and(hz == z, hc == core)
 
     my_qslot = lax.rem(z, 4) * 2 + core
     my_kslot = x * 4 + y
@@ -90,15 +93,17 @@
     for target in greeted:
         pl.semaphore_signal(barrier, inc=1, device_id=target, device_id_type=MESH)
 
-    sends = []
-
-    def send(src, dst, recv_sem, target):
-        cp = pltpu.make_async_remote_copy(
-            src_ref=src, dst_ref=dst, send_sem=send_sem.at[len(sends)], recv_sem=recv_sem,
+    def send(kind, src, dst, recv_sem, target):
+        pltpu.make_async_remote_copy(
+            src_ref=src, dst_ref=dst, send_sem=send_sem.at[kind], recv_sem=recv_sem,
             device_id=target, device_id_type=MESH,
-        )
-        sends.append(cp)
-        cp.start()
+        ).start()
+
+    def sent(kind, whole):
+        pltpu.make_async_remote_copy(
+            src_ref=whole, dst_ref=whole, send_sem=send_sem.at[kind], recv_sem=mb_recv.at[0],
+            device_id=sibling, device_id_type=MESH,
+        ).wait_send()
 
     def arrived(dst, recv_sem):
         pltpu.make_async_remote_copy(
@@ -144,33 +149,33 @@
             there = o - sign * 2
             if there in ROUND_OF:
                 send(
-                    qbuf.at[ROUND_OF[o], qslot(o), chunks[c]],
+                    CHUNK + c, qbuf.at[ROUND_OF[o], qslot(o), chunks[c]],
                     qbuf.at[ROUND_OF[there], qslot(o), chunks[c]],
-                    q_recv.at[c, there + 7], at_z(sign * 2),
+                    q_recv.at[q_index(there, c)], at_z(sign * 2),
                 )
 
     def deliver(o):
         for sign in directions(o):
             there = o - sign
             send(
-                qbuf.at[ROUND_OF[o], qslot(o)], qbuf.at[ROUND_OF[there], qslot(o)],
-                q_recv.at[1, there + 7], at_z(sign),
+                DELIVER, qbuf.at[ROUND_OF[o], qslot(o)], qbuf.at[ROUND_OF[there], qslot(o)],
+                q_recv.at[q_index(there, 1)], at_z(sign),
             )
 
     def to_sibling(o):
         ref = qbuf.at[ROUND_OF[o], qslot(o)]
-        send(ref, ref, qs_recv.at[o + 7], sibling)
+        send(SIBLING, ref, ref, qs_recv.at[ROUND_OF[o]], sibling)
 
     def take(o, c):
-        arrived(qbuf.at[ROUND_OF[o], qslot(o), chunks[c]], q_recv.at[c, o + 7])
+        arrived(qbuf.at[ROUND_OF[o], qslot(o), chunks[c]], q_recv.at[q_index(o, c)])
 
     def take_whole(o):
-        arrived(qbuf.at[ROUND_OF[o], qslot(o)], q_recv.at[1, o + 7])
+        arrived(qbuf.at[ROUND_OF[o], qslot(o)], q_recv.at[q_index(o, 1)])
 
     def keys_out(first, last):
         for i in range(first, last):
             ref = kbuf.at[my_kslot]
-            send(ref, ref, k_recv.at[i], at_plane(*PLANE[i]))
+            send(KEYS, ref, ref, k_recv.at[0], at_plane(*PLANE[i]))
 
     relay(0, 0)
     relay(0, 1)
@@ -180,15 +185,14 @@
 
     ahead = lax.rem(to_z - z + 16, 16)
     ahead = jnp.where(ahead > 8, ahead - 16, ahead)
-    last = send_sem.shape[0] - 1
 
     m_direct = pltpu.make_async_remote_copy(
-        src_ref=mrow, dst_ref=mbuf.at[my_mslot], send_sem=send_sem.at[last],
-        recv_sem=m_recv.at[my_mslot], device_id=device(x, y, to_z, to_core), device_id_type=MESH,
+        src_ref=mrow, dst_ref=mbuf.at[my_mslot], send_sem=send_sem.at[M_FIRST],
+        recv_sem=m_recv.at[0], device_id=device(x, y, to_z, to_core), device_id_type=MESH,
     )
     m_first = {
         sign: pltpu.make_async_remote_copy(
-            src_ref=mrow, dst_ref=mstage.at[2 * j + core], send_sem=send_sem.at[last],
+            src_ref=mrow, dst_ref=mstage.at[2 * j + core], send_sem=send_sem.at[M_FIRST],
             recv_sem=ms_recv.at[2 * j + core],
             device_id=device(x, y, lax.rem(z + 4 * sign + 16, 16), to_core), device_id_type=MESH,
         )
@@ -204,8 +208,8 @@
             m_onward.append((
                 jnp.logical_and(core == to_core, far * sign > 4),
                 pltpu.make_async_remote_copy(
-                    src_ref=mstage.at[2 * j + hc], dst_ref=mbuf.at[mslot], send_sem=send_sem.at[last - 16 - 2 * j - hc],
-                    recv_sem=m_recv.at[mslot], device_id=device(x, y, to_z, to_core), device_id_type=MESH,
+                    src_ref=mstage.at[2 * j + hc], dst_ref=mbuf.at[mslot], send_sem=send_sem.at[M_ONWARD + 2 * j + hc],
+                    recv_sem=m_recv.at[0], device_id=device(x, y, to_z, to_core), device_id_type=MESH,
                 ),
             ))
     m_near = jnp.logical_and(jnp.logical_not(to_self), jnp.abs(ahead) <= 4)
@@ -290,8 +294,7 @@
             block(r, 1, 1, kb, True, False, first)
 
     def ready(r):
-        for o in ROUNDS[r]:
-            arrived(qbuf.at[r, sslot(o)], qs_recv.at[o + 7])
+        arrived(qbuf.at[r, pl.ds(0, 4)], qs_recv.at[r])
         unpack(r)
 
     def stage(k):
@@ -313,7 +316,10 @@
         for i, o in enumerate(ROUNDS[r]):
             sib_out[r, i, 0:half] = dq[r, 0, sslot(o)].astype(BF16)
             sib_out[r, i, half:shard] = dq[r, 1, sslot(o)].astype(BF16)
-        send(sib_out.at[r], sib_in.at[r], sib_recv.at[r], sibling)
+        send(SHARE, sib_out.at[r], sib_in.at[r], sib_recv.at[r], sibling)
+
+    def out_slot(o):
+        return o + 7 if o < 0 else o + 6
 
     def home_far(r):
         arrived(sib_in.at[r], sib_recv.at[r])
@@ -321,37 +327,37 @@
             if o in HAND_ON or (o != 0 and o not in TAKES):
                 for h in range(2):
                     span = slice(h * half, (h + 1) * half)
-                    dq_out[r, i, span] = (dq[r, h, qslot(o)] + sib_in[r, i, span].astype(F32)).astype(BF16)
+                    dq_out[out_slot(o), span] = (dq[r, h, qslot(o)] + sib_in[r, i, span].astype(F32)).astype(BF16)
                 if o not in HAND_ON:
-                    send(dq_out.at[r, i], dq_in.at[FINAL.index(o)], dq_recv.at[FINAL.index(o)], at_z(o))
+                    send(HOME, dq_out.at[out_slot(o)], dq_in.at[FINAL.index(o)], dq_recv.at[0], at_z(o))
                 else:
                     there = HAND_ON[o]
-                    rt = ROUND_OF[there]
-                    j = ROUNDS[rt].index(there)
-                    send(dq_out.at[r, i], pair_in.at[rt, j], pair_recv.at[rt, j], at_z(o - there))
+                    j = PAIRS.index(there)
+                    send(HOME, dq_out.at[out_slot(o)], pair_in.at[j], pair_recv.at[j], at_z(o - there))
 
     def home_near(r):
         for i, o in enumerate(ROUNDS[r]):
             if o in TAKES or o == 0:
                 if o != 0:
-                    arrived(pair_in.at[r, i], pair_recv.at[r, i])
+                    j = PAIRS.index(o)
+                    arrived(pair_in.at[j], pair_recv.at[j])
                 for h in range(2):
                     span = slice(h * half, (h + 1) * half)
                     total = dq[r, h, qslot(o)] + sib_in[r, i, span].astype(F32)
                     if o == 0:
                         dq[r, h, qslot(o)] = total
                     else:
-                        dq_out[r, i, span] = (total + pair_in[r, i, span].astype(F32)).astype(BF16)
+                        dq_out[out_slot(o), span] = (total + pair_in[j, span].astype(F32)).astype(BF16)
                 if o != 0:
-                    send(dq_out.at[r, i], dq_in.at[FINAL.index(o)], dq_recv.at[FINAL.index(o)], at_z(o))
+                    send(HOME, dq_out.at[out_slot(o)], dq_in.at[FINAL.index(o)], dq_recv.at[0], at_z(o))
 
     def keys_home(h):
         for i, (a, b) in enumerate(PLANE):
             slot = lax.rem(x + a, 4) * 4 + lax.rem(y + b, 4)
             span = pl.ds(pl.multiple_of(slot * half, 16), half)
-            kv_out[i, h, 0] = dk[h, span].astype(BF16)
-            kv_out[i, h, 1] = dv[h, span].astype(BF16)
-            send(kv_out.at[i, h], kv_in.at[i, h], kv_recv.at[i, h], at_plane(a, b))
+            kv_out[h, i, 0] = dk[h, span].astype(BF16)
+            kv_out[h, i, 1] = dv[h, span].astype(BF16)
+            send(KEYS_HOME, kv_out.at[h, i], kv_in.at[h, i], kv_recv.at[h], at_plane(a, b))
 
     stage(1)
 
@@ -366,19 +372,20 @@
     stage(2)
     ready(1)
 
-    for slot in range(16):
-        hz, hc, mine = holder(slot)
-
-        @pl.when(jnp.logical_and(collects, jnp.logical_not(mine)))
-        def _():
-            arrived(mbuf.at[slot], m_recv.at[slot])
+    @pl.when(jnp.logical_and(collects, to_self))
+    def _():
+        arrived(mbuf.at[pl.ds(0, 15)], m_recv.at[0])
+
+    @pl.when(jnp.logical_and(collects, jnp.logical_not(to_self)))
+    def _():
+        arrived(mbuf, m_recv.at[0])
 
     mb_copies = [
         pltpu.make_async_remote_copy(
-            src_ref=mbuf, dst_ref=mbuf, send_sem=send_sem.at[send_sem.shape[0] - 2 - i],
+            src_ref=mbuf, dst_ref=mbuf, send_sem=send_sem.at[M_LAST],
             recv_sem=mb_recv.at[0], device_id=at_plane(a, b), device_id_type=MESH,
         )
-        for i, (a, b) in enumerate(PLANE)
+        for a, b in PLANE
     ]
 
     @pl.when(collects)
@@ -386,8 +393,7 @@
         for cp in mb_copies:
             cp.start()
 
-    for i, (a, b) in enumerate(PLANE):
-        arrived(kbuf.at[lax.rem(x - a + 4, 4) * 4 + lax.rem(y - b + 4, 4)], k_recv.at[i])
+    arrived(kbuf.at[pl.ds(0, 15)], k_recv.at[0])
     late_early(0, True)
     late_early(1, False)
     stage(3)
@@ -411,19 +417,19 @@
     late_late(1, False)
     share(1)
     home_far(0)
+    early_early(2)
     stage(4)
     home_near(0)
     home_far(1)
     ready(3)
     late_early(3, False)
     early_early(3)
+    keys_home(0)
     late_late(3, False)
     share(3)
     home_near(1)
-    early_early(2)
-    keys_home(0)
+    late_late(2, False)
     home_far(3)
-    late_late(2, False)
     share(2)
     keys_home(1)
     arrived(sib_in.at[2], sib_recv.at[2])
@@ -433,23 +439,29 @@
         span = pl.ds(pl.multiple_of(my_kslot * half, 16), half)
         rowspan = slice(h * half, (h + 1) * half)
         sk, sv = dk[h, span], dv[h, span]
+        arrived(kv_in.at[h], kv_recv.at[h])
         for i in range(15):
-            arrived(kv_in.at[i, h], kv_recv.at[i, h])
-            sk = sk + kv_in[i, h, 0].astype(F32)
-            sv = sv + kv_in[i, h, 1].astype(F32)
-        gk_ref[rowspan] = (sk * scale).astype(BF16)
-        gv_ref[rowspan] = sv.astype(BF16)
+            sk = sk + kv_in[h, i, 0].astype(F32)
+            sv = sv + kv_in[h, i, 1].astype(F32)
+        out_ref[1, rowspan] = sk
+        out_ref[2, rowspan] = sv * (1.0 / scale)
 
     totals = [dq[0, h, my_qslot] for h in range(2)]
+    arrived(dq_in, dq_recv.at[0])
     for i in range(len(FINAL)):
-        arrived(dq_in.at[i], dq_recv.at[i])
         for h in range(2):
             totals[h] = totals[h] + dq_in[i, h * half:(h + 1) * half].astype(F32)
     for h in range(2):
-        gq_ref[h * half:(h + 1) * half] = (totals[h] * scale).astype(BF16)
-
-    for cp in sends:
-        cp.wait_send()
+        out_ref[0, h * half:(h + 1) * half] = totals[h]
+
+    sent(CHUNK, qbuf.at[0, pl.ds(0, 7), chunks[0]])
+    sent(CHUNK + 1, qbuf.at[0, pl.ds(0, 7), chunks[1]])
+    sent(DELIVER, qbuf.at[0])
+    sent(SIBLING, qbuf.at[pl.ds(0, 2)])
+    sent(KEYS, kbuf.at[pl.ds(0, 15)])
+    sent(SHARE, sib_out)
+    sent(HOME, dq_out)
+    sent(KEYS_HOME, kv_out)
 
     @pl.when(m_near)
     def _():
@@ -469,8 +481,7 @@
 
     @pl.when(collects)
     def _():
-        for cp in mb_copies:
-            cp.wait_send()
+        sent(M_LAST, mwide)
 
 
 def shards(queries, key_vectors, value_vectors, outputs, out_grad, logsumexp, positions):
@@ -478,12 +489,12 @@
     half = shard // 2
     vmem = pl.BlockSpec(memory_space=pltpu.VMEM)
     dma = pltpu.SemaphoreType.DMA
-    return pl.pallas_call(
+    sums = pl.pallas_call(
         functools.partial(kernel, half),
         name="attention_backward",
-        out_shape=[jax.ShapeDtypeStruct((shard, width), BF16)] * 3,
+        out_shape=jax.ShapeDtypeStruct((3, shard, width), F32),
         in_specs=[pl.BlockSpec(memory_space=pltpu.HBM)] * 7,
-        out_specs=[vmem] * 3,
+        out_specs=vmem,
         scratch_shapes=[
             pltpu.VMEM((4, 8, 2 * shard + 16, width), BF16),
             pltpu.VMEM((16, 2 * shard, width), BF16),
@@ -494,6 +505,7 @@
             pltpu.VMEM((1, 128), F32),
             pltpu.VMEM((4, 1, 128), F32),
             pltpu.VMEM((16, 1, 128), F32),
+            pltpu.VMEM((15, 16, 1, 128), F32),
             pltpu.VMEM((2, 16 * half, 128), F32),
             pltpu.VMEM((4, 8, 8 * half), F32),
             pltpu.VMEM((4, 2, 8, half, width), F32),
@@ -501,23 +513,23 @@
             pltpu.VMEM((2, 16 * half, width), F32),
             pltpu.VMEM((4, 4, shard, width), BF16),
             pltpu.VMEM((4, 4, shard, width), BF16),
-            pltpu.VMEM((4, 4, shard, width), BF16),
-            pltpu.VMEM((4, 4, shard, width), BF16),
+            pltpu.VMEM((15, shard, width), BF16),
+            pltpu.VMEM((len(PAIRS), shard, width), BF16),
             pltpu.VMEM((len(FINAL), shard, width), BF16),
-            pltpu.VMEM((15, 2, 2, half, width), BF16),
-            pltpu.VMEM((15, 2, 2, half, width), BF16),
+            pltpu.VMEM((2, 15, 2, half, width), BF16),
+            pltpu.VMEM((2, 15, 2, half, width), BF16),
             dma((7,)),
-            dma((160,)),
-            dma((2, 16)),
-            dma((16,)),
-            dma((15,)),
+            dma((14,)),
+            dma((22,)),
             dma((4,)),
-            dma((16,)),
             dma((1,)),
             dma((4,)),
-            dma((4, 4)),
-            dma((len(FINAL),)),
-            dma((15, 2)),
+            dma((1,)),
+            dma((1,)),
+            dma((4,)),
+            dma((len(PAIRS),)),
+            dma((1,)),
+            dma((2,)),
         ],
         compiler_params=pltpu.CompilerParams(
             collective_id=0, has_side_effects=True, vmem_limit_bytes=60 * 2 ** 20
@@ -526,6 +538,8 @@
         queries, key_vectors, value_vectors, outputs, out_grad,
         logsumexp.reshape(1, shard), positions.reshape(1, shard),
     )
+    scale = width ** -0.5
+    return ((sums[0] * scale).astype(BF16), (sums[1] * scale).astype(BF16), (sums[2] * scale).astype(BF16))
 
 
 def solution(mesh):

time: 62.8 us -> 59.2 us (0.943)
  local copies, waits for them, and re-layouts: 2.71 us -> 0 us
  Pallas kernels: 59.1 us -> 56.8 us
  other arithmetic: 0 us -> 1.48 us
    unnamed x7 -> x0, local copies, waits for them, and re-layouts: 2.71 us -> none
    pallas_call x1, Pallas kernels: 59.1 us -> 56.8 us  [shards(): pl.pallas_call(functools.partial(kernel, half), name='attention_backward'...]
    convert_element_type x0 -> x1, other arithmetic: none -> 1.48 us  [shards(): (sums[2] * scale).astype(BF16)]
where the time goes in v4:
time: 59.2 us; the launch traced here: 58.9 us
  Pallas kernels  56.8 us (96%)
  other arithmetic  1.48 us (2%)
  between operations  0.64 us (1%)
    pallas_call x1, Pallas kernels, shards(): pl.pallas_call(functools.partial(kernel, half), name='attention_backward'...  56.8 us
    convert_element_type x1, other arithmetic, shards(): (sums[2] * scale).astype(BF16)  1.48 us

profile of v4, /device:TPU:8, one launch (start us, length us, event | category | flops | bytes accessed | tf_op | source)
XLA Modules:
  0.0 58.9 jit_solution(11009079653941016103)
XLA Ops:
  0.6 56.8 %attention_backward.1 = f32[3,96,128]{2,1,0:T(8,128)} custom-call(bf16[96,128]{1,0:T(8,128)(2,1)} %q_hbm.1, bf16[96,128]{1,0:T(8,128)(2,1)} %k_hbm.1, bf16[96,128]{1,0:T(8,128)(2,1)} %v_hbm.1, bf16[96,128]{1,0:T(8,128)(2,1)} %o_hbm.1, bf16[96,128]{1,0:T(8,128)(2,1)} %do_hbm.1, f32[1,96]{1,0:T(1,128)} %bitcast.8, s32[1,96]{1,0:T(1,128)} %bitcast.9), custom_call_target="tpu_custom_call" | custom-call | tf_op jit(solution)/shard_map/attention_backward/pallas_call | solution.py:492
  57.4 1.5 %fusion.2 = (bf16[96,128]{1,0:T(8,128)(2,1)}, bf16[96,128]{1,0:T(8,128)(2,1)}, bf16[96,128]{1,0:T(8,128)(2,1)}) fusion(f32[3,96,128]{2,1,0:T(8,128)} %attention_backward.1), kind=kLoop, calls=%fused_computation.5 | loop fusion | flops 73728 | bytes 221184 | tf_op jit(solution)/shard_map/convert_element_type | solution.py:542

commit v5 on v4

--- a/solution.py
+++ b/solution.py
@@ -23,8 +23,9 @@
 PLANE = (
     (2, 2), (3, 2), (2, 1), (0, 2), (1, 2), (3, 1), (2, 3), (0, 1), (1, 1), (3, 3), (1, 3), (0, 3), (2, 0), (3, 0), (1, 0),
 )
-PAIRS = tuple(sorted(set(HAND_ON.values())))
-CHUNK, DELIVER, SIBLING, KEYS, SHARE, HOME, KEYS_HOME, M_FIRST, M_LAST, M_ONWARD = 0, 2, 3, 4, 5, 6, 7, 8, 9, 10
+PAIRS = tuple(sorted(HAND_ON[o] for r in (0, 1) for o in ROUNDS[r] if o in HAND_ON))
+OUTS = tuple(o for r in (0, 1, 2) for o in ROUNDS[r] if o != 0)
+CHUNK, DELIVER, SIBLING, KEYS, SHARE, HOME, KEYS_HOME, M_FIRST, M_LAST, OUTERMOST, M_ONWARD = 0, 2, 3, 4, 5, 6, 7, 8, 9, 10, 11
 
 
 def q_index(o, c):
@@ -43,8 +44,8 @@
     half, q_hbm, k_hbm, v_hbm, o_hbm, do_hbm, lse_hbm, pos_hbm,
     out_ref,
     qbuf, kbuf, o_ref, lse_ref, pos_ref, rowbuf, mrow, mstage, mbuf, mwide, pk, rows, dq, dk, dv,
-    sib_out, sib_in, dq_out, pair_in, dq_in, kv_out, kv_in,
-    in_sem, send_sem, q_recv, qs_recv, k_recv, ms_recv, m_recv, mb_recv, sib_recv, pair_recv, dq_recv, kv_recv,
+    sib_out, sib_in, dq_out, outer_out, pair_in, outer_in, dq_in, kv_out, kv_in,
+    in_sem, send_sem, q_recv, qs_recv, k_recv, ms_recv, m_recv, mb_recv, sib_recv, pair_recv, outer_recv, dq_recv, kv_recv,
 ):
     width = q_hbm.shape[1]
     shard = 2 * half
@@ -297,6 +298,11 @@
         arrived(qbuf.at[r, pl.ds(0, 4)], qs_recv.at[r])
         unpack(r)
 
+    def nearby(k):
+        for o in (-2 * k + 1, 2 * k - 1):
+            take_whole(o)
+            to_sibling(o)
+
     def stage(k):
         far = [o for o in (-2 * k, 2 * k) if o in ROUND_OF]
         for c in range(2):
@@ -308,9 +314,8 @@
             if k < 4:
                 deliver(o)
             to_sibling(o)
-        for o in (-2 * k + 1, 2 * k - 1):
-            take_whole(o)
-            to_sibling(o)
+        if k < 4:
+            nearby(k)
 
     def share(r):
         for i, o in enumerate(ROUNDS[r]):
@@ -319,7 +324,19 @@
         send(SHARE, sib_out.at[r], sib_in.at[r], sib_recv.at[r], sibling)
 
     def out_slot(o):
-        return o + 7 if o < 0 else o + 6
+        return OUTS.index(o)
+
+    def home_outermost():
+        for i, o in reversed(tuple(enumerate(ROUNDS[3]))):
+            j = ROUNDS[2].index(HAND_ON[o])
+            nearer = lax.rem(z + o - HAND_ON[o] + 16, 16)
+            for n, (slot, to) in enumerate(((qslot(o), core), (sslot(o), other))):
+                for h in range(2):
+                    outer_out[2 * i + n, h * half:(h + 1) * half] = dq[3, h, slot].astype(BF16)
+                send(
+                    OUTERMOST, outer_out.at[2 * i + n], outer_in.at[j, n], outer_recv.at[j],
+                    device(x, y, nearer, to),
+                )
 
     def home_far(r):
         arrived(sib_in.at[r], sib_recv.at[r])
@@ -336,18 +353,25 @@
                     send(HOME, dq_out.at[out_slot(o)], pair_in.at[j], pair_recv.at[j], at_z(o - there))
 
     def home_near(r):
-        for i, o in enumerate(ROUNDS[r]):
+        for i, o in reversed(tuple(enumerate(ROUNDS[r]))):
             if o in TAKES or o == 0:
                 if o != 0:
-                    j = PAIRS.index(o)
-                    arrived(pair_in.at[j], pair_recv.at[j])
+                    if r == 2:
+                        arrived(outer_in.at[i], outer_recv.at[i])
+                    else:
+                        j = PAIRS.index(o)
+                        arrived(pair_in.at[j], pair_recv.at[j])
                 for h in range(2):
                     span = slice(h * half, (h + 1) * half)
                     total = dq[r, h, qslot(o)] + sib_in[r, i, span].astype(F32)
                     if o == 0:
                         dq[r, h, qslot(o)] = total
                     else:
-                        dq_out[out_slot(o), span] = (total + pair_in[j, span].astype(F32)).astype(BF16)
+                        if r == 2:
+                            more = outer_in[i, 0, span].astype(F32) + outer_in[i, 1, span].astype(F32)
+                        else:
+                            more = pair_in[j, span].astype(F32)
+                        dq_out[out_slot(o), span] = (total + more).astype(BF16)
                 if o != 0:
                     send(HOME, dq_out.at[out_slot(o)], dq_in.at[FINAL.index(o)], dq_recv.at[0], at_z(o))
 
@@ -418,20 +442,20 @@
     share(1)
     home_far(0)
     early_early(2)
+    nearby(4)
     stage(4)
     home_near(0)
     home_far(1)
     ready(3)
     late_early(3, False)
     early_early(3)
+    late_late(3, False)
+    home_outermost()
     keys_home(0)
-    late_late(3, False)
-    share(3)
-    home_near(1)
     late_late(2, False)
-    home_far(3)
     share(2)
     keys_home(1)
+    home_near(1)
     arrived(sib_in.at[2], sib_recv.at[2])
     home_near(2)
 
@@ -461,6 +485,7 @@
     sent(KEYS, kbuf.at[pl.ds(0, 15)])
     sent(SHARE, sib_out)
     sent(HOME, dq_out)
+    sent(OUTERMOST, outer_out)
     sent(KEYS_HOME, kv_out)
 
     @pl.when(m_near)
@@ -492,7 +517,7 @@
     sums = pl.pallas_call(
         functools.partial(kernel, half),
         name="attention_backward",
-        out_shape=jax.ShapeDtypeStruct((3, shard, width), F32),
+        out_shape=pltpu.VMEM((3, shard, width), F32),
         in_specs=[pl.BlockSpec(memory_space=pltpu.HBM)] * 7,
         out_specs=vmem,
         scratch_shapes=[
@@ -511,23 +536,26 @@
             pltpu.VMEM((4, 2, 8, half, width), F32),
             pltpu.VMEM((2, 16 * half, width), F32),
             pltpu.VMEM((2, 16 * half, width), F32),
-            pltpu.VMEM((4, 4, shard, width), BF16),
-            pltpu.VMEM((4, 4, shard, width), BF16),
-            pltpu.VMEM((15, shard, width), BF16),
+            pltpu.VMEM((3, 4, shard, width), BF16),
+            pltpu.VMEM((3, 4, shard, width), BF16),
+            pltpu.VMEM((len(OUTS), shard, width), BF16),
+            pltpu.VMEM((8, shard, width), BF16),
             pltpu.VMEM((len(PAIRS), shard, width), BF16),
+            pltpu.VMEM((4, 2, shard, width), BF16),
             pltpu.VMEM((len(FINAL), shard, width), BF16),
             pltpu.VMEM((2, 15, 2, half, width), BF16),
             pltpu.VMEM((2, 15, 2, half, width), BF16),
             dma((7,)),
-            dma((14,)),
+            dma((15,)),
             dma((22,)),
             dma((4,)),
             dma((1,)),
             dma((4,)),
             dma((1,)),
             dma((1,)),
+            dma((3,)),
+            dma((len(PAIRS),)),
             dma((4,)),
-            dma((len(PAIRS),)),
             dma((1,)),
             dma((2,)),
         ],

time: 59.2 us -> 56.8 us (0.959)
  the two profiles are of different devices: /device:TPU:8 before, /device:TPU:1 now
where the time goes in v5:
time: 56.8 us; the launch traced here: 56.7 us
  Pallas kernels  55.4 us (98%)
  between operations  0.64 us (1%)
  other arithmetic  0.63 us (1%)
    pallas_call x1, Pallas kernels, shards(): pl.pallas_call(functools.partial(kernel, half), name='attention_backward'...  55.4 us

profile of v5, /device:TPU:1, one launch (start us, length us, event | category | flops | bytes accessed | tf_op | source)
XLA Modules:
  0.0 56.7 jit_solution(9802369725939307681)
XLA Ops:
  0.6 55.4 %attention_backward.1 = f32[3,96,128]{2,1,0:T(8,128)S(1)} custom-call(bf16[96,128]{1,0:T(8,128)(2,1)} %q_hbm.1, bf16[96,128]{1,0:T(8,128)(2,1)} %k_hbm.1, bf16[96,128]{1,0:T(8,128)(2,1)} %v_hbm.1, bf16[96,128]{1,0:T(8,128)(2,1)} %o_hbm.1, bf16[96,128]{1,0:T(8,128)(2,1)} %do_hbm.1, f32[1,96]{1,0:T(1,128)} %bitcast.8, s32[1,96]{1,0:T(1,128)} %bitcast.9), custom_call_target="tpu_custom_call" | custom-call | tf_op jit(solution)/shard_map/attention_backward/pallas_call | solution.py:517
  56.0 0.6 %fusion.2 = (bf16[96,128]{1,0:T(8,128)(2,1)}, bf16[96,128]{1,0:T(8,128)(2,1)}, bf16[96,128]{1,0:T(8,128)(2,1)}) fusion(f32[3,96,128]{2,1,0:T(8,128)S(1)} %attention_backward.1), kind=kLoop, calls=%fused_computation.5 | loop fusion | flops 73728 | bytes 221184 | tf_op jit(solution)/shard_map/convert_element_type | solution.py:570

commit v6 on v5

--- a/solution.py
+++ b/solution.py
@@ -25,11 +25,13 @@
 )
 PAIRS = tuple(sorted(HAND_ON[o] for r in (0, 1) for o in ROUNDS[r] if o in HAND_ON))
 OUTS = tuple(o for r in (0, 1, 2) for o in ROUNDS[r] if o != 0)
-CHUNK, DELIVER, SIBLING, KEYS, SHARE, HOME, KEYS_HOME, M_FIRST, M_LAST, OUTERMOST, M_ONWARD = 0, 2, 3, 4, 5, 6, 7, 8, 9, 10, 11
+CUTS = (0, 64, 128, 208)
+CHUNKS = len(CUTS) - 1
+DELIVER, SIBLING, KEYS, SHARE, HOME, KEYS_HOME, M_FIRST, M_LAST, OUTERMOST, M_ONWARD, CHUNK = 0, 1, 2, 3, 4, 5, 6, 7, 8, 9, 13
 
 
 def q_index(o, c):
-    return (o + 7) // 2 if o % 2 else 8 + (o // 2 + (3 if o < 0 else 2)) * 2 + c
+    return (o + 7) // 2 if o % 2 else 8 + (o // 2 + (3 if o < 0 else 2)) * CHUNKS + c
 
 
 def dot(a, b, dims):
@@ -140,7 +142,7 @@
     def sslot(o):
         return lax.rem(z + o + 16, 4) * 2 + other
 
-    chunks = (pl.ds(0, shard), pl.ds(shard, shard + 16))
+    chunks = tuple(pl.ds(a, b - a) for a, b in zip(CUTS, CUTS[1:]))
 
     def directions(o):
         return (1, -1) if o == 0 else ((1,) if o < 0 else (-1,))
@@ -178,8 +180,8 @@
             ref = kbuf.at[my_kslot]
             send(KEYS, ref, ref, k_recv.at[0], at_plane(*PLANE[i]))
 
-    relay(0, 0)
-    relay(0, 1)
+    for c in range(CHUNKS):
+        relay(0, c)
     to_sibling(0)
     deliver(0)
     keys_out(0, 15)
@@ -305,7 +307,7 @@
 
     def stage(k):
         far = [o for o in (-2 * k, 2 * k) if o in ROUND_OF]
-        for c in range(2):
+        for c in range(CHUNKS):
             for o in far:
                 take(o, c)
                 if k < 4:
@@ -478,8 +480,8 @@
     for h in range(2):
         out_ref[0, h * half:(h + 1) * half] = totals[h]
 
-    sent(CHUNK, qbuf.at[0, pl.ds(0, 7), chunks[0]])
-    sent(CHUNK + 1, qbuf.at[0, pl.ds(0, 7), chunks[1]])
+    for c in range(CHUNKS):
+        sent(CHUNK + c, qbuf.at[0, pl.ds(0, 7), chunks[c]])
     sent(DELIVER, qbuf.at[0])
     sent(SIBLING, qbuf.at[pl.ds(0, 2)])
     sent(KEYS, kbuf.at[pl.ds(0, 15)])
@@ -546,8 +548,8 @@
             pltpu.VMEM((2, 15, 2, half, width), BF16),
             pltpu.VMEM((2, 15, 2, half, width), BF16),
             dma((7,)),
-            dma((15,)),
-            dma((22,)),
+            dma((CHUNK + CHUNKS,)),
+            dma((8 + 7 * CHUNKS,)),
             dma((4,)),
             dma((1,)),
             dma((4,)),

time: 56.8 us -> 56.5 us (level)
  no operation moved by 1% of the time
where the time goes in v6:
time: 56.5 us; the launch traced here: 56.3 us
  Pallas kernels  55 us (97%)
  between operations  0.64 us (1%)
  other arithmetic  0.63 us (1%)
    pallas_call x1, Pallas kernels, shards(): pl.pallas_call(functools.partial(kernel, half), name='attention_backward'...  55 us

profile of v6, /device:TPU:1, one launch (start us, length us, event | category | flops | bytes accessed | tf_op | source)
XLA Modules:
  0.0 56.3 jit_solution(6289864834838978372)
XLA Ops:
  0.6 55.0 %attention_backward.1 = f32[3,96,128]{2,1,0:T(8,128)S(1)} custom-call(bf16[96,128]{1,0:T(8,128)(2,1)} %q_hbm.1, bf16[96,128]{1,0:T(8,128)(2,1)} %k_hbm.1, bf16[96,128]{1,0:T(8,128)(2,1)} %v_hbm.1, bf16[96,128]{1,0:T(8,128)(2,1)} %o_hbm.1, bf16[96,128]{1,0:T(8,128)(2,1)} %do_hbm.1, f32[1,96]{1,0:T(1,128)} %bitcast.8, s32[1,96]{1,0:T(1,128)} %bitcast.9), custom_call_target="tpu_custom_call" | custom-call | tf_op jit(solution)/shard_map/attention_backward/pallas_call | solution.py:519
  55.7 0.6 %fusion.2 = (bf16[96,128]{1,0:T(8,128)(2,1)}, bf16[96,128]{1,0:T(8,128)(2,1)}, bf16[96,128]{1,0:T(8,128)(2,1)}) fusion(f32[3,96,128]{2,1,0:T(8,128)S(1)} %attention_backward.1), kind=kLoop, calls=%fused_computation.5 | loop fusion | flops 73728 | bytes 221184 | tf_op jit(solution)/shard_map/convert_element_type | solution.py:572
